TPU v7x, 512 devices: a whole 4x4x16 slice. The times are simulated.
512 devices in a mesh: curve: 128 (over y, z, core), oct: 4 (over x).
Axes of the slice: x: 4, y: 4, z: 16, core: 2. Of those that a mesh axis runs over, the one named last changes fastest.
Arguments:
- leaf_mult: bfloat16 [152, 1048576], P(None, ('curve', 'oct')), may hold values from -6 to 6
- occupancy: int32 [1048576], P(('curve', 'oct')), may hold values from 0 to 64, as said below
- ghost_rows: int32 [6, 131072], P(None, ('curve', 'oct')), may hold values from 0 to 2047
- m2l_list: int32 [32, 1048576], P(None, ('curve', 'oct')), may hold values from 0 to 3584
- par_code: int32 [131072], P(('curve', 'oct')), may hold values from 0 to 7
- coarse_of: int32 [131072], P(('curve', 'oct')), may hold values from 0 to 63, as said below
- coarse_list: int32 [32, 64], replicated, may hold values from 0 to 64
- m2m: bfloat16 [8, 152, 152], replicated, may hold values from -0.15625 to 0.15625
- coarse_up: bfloat16 [8, 152, 152], replicated, may hold values from -0.009765625 to 0.009765625
- m2l: bfloat16 [32, 152, 152], replicated, may hold values from -0.078125 to 0.078125
- l2l: bfloat16 [8, 152, 152], replicated, may hold values from -0.5 to 0.5
Outputs:
- leaf_local: bfloat16 [152, 1048576], P(None, ('curve', 'oct'))
Inputs may be any that keep to these rules, and one draw needn't show every extreme that they name: `occupancy`: on each device the slots with sources come first and the rest are empty; the number of occupied slots differs from device to device and some device is full. `m2l_list`: entries 2048 + k * 256 + t name column t of ghost block k; the largest value names the zero column. `coarse_of`: never falls by more than two along the parents. `coarse_list`: the value 64 means no partner.
All inputs are finite; a program needn't handle non-finite values.
Results may differ from a plain program's by a relative error of at most 0.01.
Values may be sent and summed in bfloat16 or wider, within the bound.
No kernel may reach another device: no remote copies, remote signals or barrier semaphores. Data moves between devices by JAX's collectives and lax.ppermute only.
A program may use at most 64 MiB of HBM per device.

v0:
```python
import jax
import jax.numpy as jnp
from jax import lax
from jax.sharding import PartitionSpec as P

REACH = 3
COARSE = 64


def passed_along(block, axis, distance):
    devices = range(lax.axis_size(axis))
    route = [(i - distance, i) for i in devices if i - distance in devices]
    return lax.ppermute(block, axis, route)


def translate_sum(operators, lists, source_rows, columns):
    points = operators.shape[1]
    groups = operators.shape[0] // 8
    grouped_ops = operators.reshape(groups, 8, points, points)
    grouped_idx = lists.reshape(groups, 8, columns)

    def group_step(running, operands):
        operator, column = operands
        gathered = jnp.take(source_rows, column, axis=0)
        return (
            running
            + jnp.einsum("rpq,rbq->pb", operator, gathered, preferred_element_type=jnp.float32),
            None,
        )

    total, _ = lax.scan(
        group_step, jnp.zeros((points, columns), jnp.float32), (grouped_ops, grouped_idx)
    )
    return total


def shards(
    leaf_mult,
    occupancy,
    ghost_rows,
    m2l_list,
    par_code,
    coarse_of,
    coarse_list,
    m2m,
    coarse_up,
    m2l,
    l2l,
):
    points, slots = leaf_mult.shape
    parents = slots // 8
    stride_list = [stride for stride in range(-REACH, REACH + 1) if stride != 0]
    scaled = occupancy.astype(jnp.float32) * 0.03125
    charged = (leaf_mult.astype(jnp.float32) * scaled[None, :]).astype(jnp.bfloat16)
    charged_rows = charged.T
    packets = [
        jnp.take(charged_rows, ghost_rows[position], axis=0) for position in range(2 * REACH)
    ]
    by_stride = {}
    for position, stride in enumerate(stride_list):
        by_stride[stride] = passed_along(packets[position], "curve", stride)
    blocks = [by_stride[stride] for stride in stride_list]
    extended = jnp.concatenate(
        [charged_rows] + blocks + [jnp.zeros((1, points), jnp.bfloat16)], axis=0
    )
    leaf_far = translate_sum(m2l, m2l_list, extended, slots)
    children = charged.reshape(points, parents, 8)
    parent_mult = jnp.einsum(
        "kpq,qbk->pb", m2m, children, preferred_element_type=jnp.float32
    ).astype(jnp.bfloat16)
    codes = jnp.arange(8, dtype=jnp.int32)
    selected = par_code[None, :] == codes[:, None]
    stacked = jnp.where(selected[:, None, :], parent_mult[None], jnp.zeros((), jnp.bfloat16))
    lifted = jnp.einsum("kpq,kqb->pb", coarse_up, stacked, preferred_element_type=jnp.float32)
    member = (coarse_of[:, None] == jnp.arange(COARSE, dtype=jnp.int32)[None, :]).astype(
        jnp.float32
    )
    partial_sum = jnp.dot(lifted, member, precision=lax.Precision.HIGHEST)
    coarse_mult = lax.psum(partial_sum, ("curve", "oct")).astype(jnp.bfloat16)
    coarse_ext = jnp.concatenate([coarse_mult.T, jnp.zeros((1, points), jnp.bfloat16)], axis=0)
    coarse_acc = translate_sum(m2l, coarse_list, coarse_ext, COARSE)
    coarse_local = coarse_acc.astype(jnp.bfloat16)
    pulled = jnp.take(coarse_local, coarse_of, axis=1)
    stacked_down = jnp.where(selected[:, None, :], pulled[None], jnp.zeros((), jnp.bfloat16))
    parent_local = jnp.einsum(
        "kpq,kqb->pb", l2l, stacked_down, preferred_element_type=jnp.float32
    ).astype(jnp.bfloat16)
    descended = jnp.einsum(
        "kpq,qb->pbk", l2l, parent_local, preferred_element_type=jnp.float32
    ).reshape(points, slots)
    result = jnp.where((occupancy > 0)[None, :], leaf_far + descended, jnp.float32(0.0))
    return result.astype(jnp.bfloat16)


def solution(mesh):
    placed = (
        P(None, ("curve", "oct")),
        P(("curve", "oct")),
        P(None, ("curve", "oct")),
        P(None, ("curve", "oct")),
        P(("curve", "oct")),
        P(("curve", "oct")),
        P(),
        P(),
        P(),
        P(),
        P(),
    )
    return jax.shard_map(
        shards, mesh=mesh, in_specs=placed, out_specs=P(None, ("curve", "oct")), check_vma=False
    )
```

profile of v0, /device:TPU:1, one launch (start us, length us, event | category | flops | bytes accessed | tf_op | source)
XLA Modules:
  0.0 513.0 jit_solution(6823562063210989476)
XLA Ops:
  1.0 2.2 copy.22
  18.4 8.8 %collective-permute-start.2 = (bf16[256,152]{1,0:T(8,128)(2,1)}, bf16[256,152]{1,0:T(8,128)(2,1)}, u32[]{:S(2)}, u32[]{:S(2)}) collective-permute-start(bf16[256,152]{1,0:T(8,128)(2,1)} %broadcast_select_fusion.3), channel_id=1, source_target_pairs={{4,0},{8,4},{12,8},{16,12},{20,16},{24,20},{28,24},{32,28},{36,32}... | collective-permute-start | bytes 233480 | tf_op jit(solution)/shard_map/ppermute | solution.py:13
  30.7 4.3 collective-permute-start.3
  38.5 4.6 collective-permute-start.4
  43.2 2.5 fusion.34
  50.3 106.4 %psum.7 = bf16[152,64]{0,1:T(8,128)(2,1)S(1)} all-reduce(f32[152,64]{0,1:T(8,128)S(1)} %fusion.42), channel_id=1, replica_groups=mesh['curve'=128,'oct'=4] {'curve','oct'}, use_global_device_ids=true, to_apply=%region_2.4 | all-reduce | flops 9728 | bytes 58368 | tf_op jit(solution)/shard_map/psum | solution.py:79
  156.7 14.3 %while.23 = (s32[]{:T(128)}, f32[152,64]{0,1:T(8,128)S(1)}, bf16[4,8,152,152]{3,2,1,0:T(8,128)(2,1)}, s32[4,8,64]{2,1,0:T(8,128)S(1)}, bf16[65,152]{1,0:T(8,128)(2,1)S(1)}, /*index=5*/s32[]{:T(128)}, s32[]{:T(128)}) while((s32[]{:T(128)}, f32[152,64]{0,1:T(8,128)S(1)}, bf16[4,8,152,152]{3,2,1,0:T(8,128)(2,1)}, ...), condition=%wide.region_4.6_spmd.clone, body=%wide.region_3.5_spmd.clone.sunk | while | flops 23761412 | bytes 1187423 | solution.py:31
  174.4 2.9 copy.25
  177.3 2.7 copy.26
  180.0 2.4 collective-permute-start.5
  187.1 323.2 %while.22 = (s32[]{:T(128)}, f32[152,2048]{1,0:T(8,128)}, bf16[4,8,152,152]{3,2,1,0:T(8,128)(2,1)}, s32[4,8,2048]{2,1,0:T(8,128)S(1)}, bf16[3585,152]{1,0:T(8,128)(2,1)S(1)}, /*index=5*/s32[]{:T(128)}, s32[]{:T(128)}) while((s32[]{:T(128)}, f32[152,2048]{1,0:T(8,128)}, bf16[4,8,152,152]{3,2,1,0:T(8,128)(2,1)}, ...), condition=%wide.region_1.3_spmd.clone, body=%wide.region_0.0_spmd.clone.sunk | while | flops 760348672 | bytes 28574300 | solution.py:31
  187.2 64.8 %gather_fusion = bf16[16384,152]{1,0:T(8,128)(2,1)} fusion(bf16[3585,152]{1,0:T(8,128)(2,1)S(1)} %get-tuple-element.212, s32[16384]{0:T(1024)S(1)} %broadcast_clamp_fusion.2), kind=kCustom, calls=%fused_computation.1.clone.clone.1 | custom fusion | bytes 10027008 | tf_op jit(solution)/shard_map/while/body/eval_jaxpr/jit(_take)/gather | solution.py:24
  252.0 10.7 %copy.33 = bf16[8,2048,152]{1,2,0:T(8,128)(2,1)} copy(bf16[8,2048,152]{2,1,0:T(8,128)(2,1)} %bitcast.107) | data formatting | bytes 9961472 | tf_op jit(solution)/shard_map/while/body/eval_jaxpr/jit(_take)/gather | solution.py:24
  262.7 4.9 fusion.64
  267.7 64.8 %gather_fusion = bf16[16384,152]{1,0:T(8,128)(2,1)} fusion(bf16[3585,152]{1,0:T(8,128)(2,1)S(1)} %get-tuple-element.212, s32[16384]{0:T(1024)S(1)} %broadcast_clamp_fusion.2), kind=kCustom, calls=%fused_computation.1.clone.clone.1 | custom fusion | bytes 10027008 | tf_op jit(solution)/shard_map/while/body/eval_jaxpr/jit(_take)/gather | solution.py:24
  332.5 10.7 %copy.33 = bf16[8,2048,152]{1,2,0:T(8,128)(2,1)} copy(bf16[8,2048,152]{2,1,0:T(8,128)(2,1)} %bitcast.107) | data formatting | bytes 9961472 | tf_op jit(solution)/shard_map/while/body/eval_jaxpr/jit(_take)/gather | solution.py:24
  343.3 5.3 %fusion.64 = f32[152,2048]{1,0:T(8,128)} fusion(bf16[8,2048,152]{1,2,0:T(8,128)(2,1)} %copy.33, pred[8,2048]{1,0:T(8,128)(4,1)S(1)} %compare_and_fusion.11, f32[152,2048]{1,0:T(8,128)} %get-tuple-element.202, bf16[4,8,152,152]{3,2,1,0:T(8,128)(2,1)} %get-tuple-element.210, s32[]{:T(128)} %get-tuple-element.201, pred[]{:T(512)S(6)} %compare.7), kind=kOutput, calls=%fused_computation.14.clone.1 | convolution fusion | flops 760184832 | bytes 8110593 | tf_op jit(solution)/shard_map/while/body/eval_jaxpr/rpq,rbq->pb/dot_general | solution.py:27
  348.6 64.8 %gather_fusion = bf16[16384,152]{1,0:T(8,128)(2,1)} fusion(bf16[3585,152]{1,0:T(8,128)(2,1)S(1)} %get-tuple-element.212, s32[16384]{0:T(1024)S(1)} %broadcast_clamp_fusion.2), kind=kCustom, calls=%fused_computation.1.clone.clone.1 | custom fusion | bytes 10027008 | tf_op jit(solution)/shard_map/while/body/eval_jaxpr/jit(_take)/gather | solution.py:24
  413.4 10.7 %copy.33 = bf16[8,2048,152]{1,2,0:T(8,128)(2,1)} copy(bf16[8,2048,152]{2,1,0:T(8,128)(2,1)} %bitcast.107) | data formatting | bytes 9961472 | tf_op jit(solution)/shard_map/while/body/eval_jaxpr/jit(_take)/gather | solution.py:24
  424.1 5.3 %fusion.64 = f32[152,2048]{1,0:T(8,128)} fusion(bf16[8,2048,152]{1,2,0:T(8,128)(2,1)} %copy.33, pred[8,2048]{1,0:T(8,128)(4,1)S(1)} %compare_and_fusion.11, f32[152,2048]{1,0:T(8,128)} %get-tuple-element.202, bf16[4,8,152,152]{3,2,1,0:T(8,128)(2,1)} %get-tuple-element.210, s32[]{:T(128)} %get-tuple-element.201, pred[]{:T(512)S(6)} %compare.7), kind=kOutput, calls=%fused_computation.14.clone.1 | convolution fusion | flops 760184832 | bytes 8110593 | tf_op jit(solution)/shard_map/while/body/eval_jaxpr/rpq,rbq->pb/dot_general | solution.py:27
  429.5 64.8 %gather_fusion = bf16[16384,152]{1,0:T(8,128)(2,1)} fusion(bf16[3585,152]{1,0:T(8,128)(2,1)S(1)} %get-tuple-element.212, s32[16384]{0:T(1024)S(1)} %broadcast_clamp_fusion.2), kind=kCustom, calls=%fused_computation.1.clone.clone.1 | custom fusion | bytes 10027008 | tf_op jit(solution)/shard_map/while/body/eval_jaxpr/jit(_take)/gather | solution.py:24
  494.3 10.7 %copy.33 = bf16[8,2048,152]{1,2,0:T(8,128)(2,1)} copy(bf16[8,2048,152]{2,1,0:T(8,128)(2,1)} %bitcast.107) | data formatting | bytes 9961472 | tf_op jit(solution)/shard_map/while/body/eval_jaxpr/jit(_take)/gather | solution.py:24
  505.0 5.3 %fusion.64 = f32[152,2048]{1,0:T(8,128)} fusion(bf16[8,2048,152]{1,2,0:T(8,128)(2,1)} %copy.33, pred[8,2048]{1,0:T(8,128)(4,1)S(1)} %compare_and_fusion.11, f32[152,2048]{1,0:T(8,128)} %get-tuple-element.202, bf16[4,8,152,152]{3,2,1,0:T(8,128)(2,1)} %get-tuple-element.210, s32[]{:T(128)} %get-tuple-element.201, pred[]{:T(512)S(6)} %compare.7), kind=kOutput, calls=%fused_computation.14.clone.1 | convolution fusion | flops 760184832 | bytes 8110593 | tf_op jit(solution)/shard_map/while/body/eval_jaxpr/rpq,rbq->pb/dot_general | solution.py:27
  510.3 2.7 select_convert_fusion
  (119 shorter events, 49.9 us)
Async XLA Ops:
  0.0 172.5 %copy-start = (bf16[8,152,152]{2,1,0:T(8,128)(2,1)S(1)}, bf16[8,152,152]{2,1,0:T(8,128)(2,1)}, u32[]{:S(2)}) copy-start(bf16[8,152,152]{2,1,0:T(8,128)(2,1)} %param.27) | copy-start | bytes 1108996
  8.9 171.1 %collective-permute-start = (bf16[256,152]{1,0:T(8,128)(2,1)}, bf16[256,152]{1,0:T(8,128)(2,1)}, u32[]{:S(2)}, u32[]{:S(2)}) collective-permute-start(bf16[256,152]{1,0:T(8,128)(2,1)} %broadcast_select_fusion.5), channel_id=1, source_target_pairs={{12,0},{16,4},{20,8},{24,12},{28,16},{32,20},{36,24},{40,28},{44,3... | collective-permute-start | bytes 233480 | tf_op jit(solution)/shard_map/ppermute | solution.py:13
  13.6 169.7 %collective-permute-start.1 = (bf16[256,152]{1,0:T(8,128)(2,1)}, bf16[256,152]{1,0:T(8,128)(2,1)}, u32[]{:S(2)}, u32[]{:S(2)}) collective-permute-start(bf16[256,152]{1,0:T(8,128)(2,1)} %broadcast_select_fusion.4), channel_id=1, source_target_pairs={{8,0},{12,4},{16,8},{20,12},{24,16},{28,20},{32,24},{36,28},{40,32... | collective-permute-start | bytes 233480 | tf_op jit(solution)/shard_map/ppermute | solution.py:13
  18.4 165.8 %collective-permute-start.2 = (bf16[256,152]{1,0:T(8,128)(2,1)}, bf16[256,152]{1,0:T(8,128)(2,1)}, u32[]{:S(2)}, u32[]{:S(2)}) collective-permute-start(bf16[256,152]{1,0:T(8,128)(2,1)} %broadcast_select_fusion.3), channel_id=1, source_target_pairs={{4,0},{8,4},{12,8},{16,12},{20,16},{24,20},{28,24},{32,28},{36,32}... | collective-permute-start | bytes 233480 | tf_op jit(solution)/shard_map/ppermute | solution.py:13
  30.7 15.0 %copy-start.6 = (s32[256]{0:T(256)S(1)}, s32[256]{0:T(256)}, u32[]{:S(2)}) copy-start(s32[256]{0:T(256)} %param.22) | copy-start | bytes 3076
  30.7 154.5 %collective-permute-start.3 = (bf16[256,152]{1,0:T(8,128)(2,1)}, bf16[256,152]{1,0:T(8,128)(2,1)}, u32[]{:S(2)}, u32[]{:S(2)}) collective-permute-start(bf16[256,152]{1,0:T(8,128)(2,1)} %broadcast_select_fusion.2), channel_id=1, source_target_pairs={{0,4},{4,8},{8,12},{12,16},{16,20},{20,24},{24,28},{28,32},{32,36}... | collective-permute-start | bytes 233480 | tf_op jit(solution)/shard_map/ppermute | solution.py:13
  36.9 10.7 %copy-start.7 = (s32[256]{0:T(256)S(1)}, s32[256]{0:T(256)}, u32[]{:S(2)}) copy-start(s32[256]{0:T(256)} %param.21) | copy-start | bytes 3076
  38.5 147.6 %collective-permute-start.4 = (bf16[256,152]{1,0:T(8,128)(2,1)}, bf16[256,152]{1,0:T(8,128)(2,1)}, u32[]{:S(2)}, u32[]{:S(2)}) collective-permute-start(bf16[256,152]{1,0:T(8,128)(2,1)} %broadcast_select_fusion.1), channel_id=1, source_target_pairs={{0,8},{4,12},{8,16},{12,20},{16,24},{20,28},{24,32},{28,36},{32,40... | collective-permute-start | bytes 233480 | tf_op jit(solution)/shard_map/ppermute | solution.py:13
  47.5 2.0 copy-start.8
  47.6 109.1 %copy-start.3 = (s32[32,64]{1,0:T(8,128)S(1)}, s32[32,64]{1,0:T(8,128)}, u32[]{:S(2)}) copy-start(s32[32,64]{1,0:T(8,128)} %param.23) | copy-start | bytes 24580
  47.6 109.1 %copy-start.4 = (f32[152,64]{0,1:T(8,128)S(1)}, f32[152,64]{0,1:T(8,128)}, u32[]{:S(2)}) copy-start(f32[152,64]{0,1:T(8,128)} %custom-call.1) | copy-start | bytes 116740
  156.7 15.7 %copy-start.2 = (bf16[256,152]{1,0:T(8,128)(2,1)S(1)}, bf16[256,152]{1,0:T(8,128)(2,1)}, u32[]{:S(2)}) copy-start(bf16[256,152]{1,0:T(8,128)(2,1)} %gather_fusion.8) | copy-start | bytes 233476
  171.0 3.4 copy-start.5
  177.3 9.8 %copy-start.1 = (s32[32,2048]{1,0:T(8,128)S(1)}, s32[32,2048]{1,0:T(8,128)}, u32[]{:S(2)}) copy-start(s32[32,2048]{1,0:T(8,128)} %param.20) | copy-start | bytes 786436
  180.0 7.1 %collective-permute-start.5 = (bf16[256,152]{1,0:T(8,128)(2,1)S(1)}, bf16[256,152]{1,0:T(8,128)(2,1)S(1)}, u32[]{:S(2)}, u32[]{:S(2)}) collective-permute-start(bf16[256,152]{1,0:T(8,128)(2,1)S(1)} %broadcast_select_fusion), channel_id=1, source_target_pairs={{0,12},{4,16},{8,20},{12,24},{16,28},{20,32},{24,36},{28,40},{32,4... | collective-permute-start | bytes 233480 | tf_op jit(solution)/shard_map/ppermute | solution.py:13
where the time goes:
time: 517 us; the launch traced here: 513 us
  local copies, waits for them, and re-layouts  336 us (65%)
  blocking collectives  106 us (21%)
  matrix products  31.1 us (6%)
  starting transfers between devices  22.7 us (4%)
  other arithmetic  16.4 us (3%)
    gather x12, local copies, waits for them, and re-layouts, group_step(): gathered = jnp.take(source_rows, column, axis=0)  310 us
    psum x1, blocking collectives, shards(): coarse_mult = lax.psum(partial_sum, ('curve', 'oct')).astype(jnp.bfloat16)  106 us
    dot_general x8, matrix products, group_step(): jnp.einsum('rpq,rbq->pb', operator, gathered, preferred_element_type=jnp....  26.6 us
    ppermute x6, starting transfers between devices, passed_along(): return lax.ppermute(block, axis, route)  22.7 us
    gather x6, local copies, waits for them, and re-layouts, shards(): jnp.take(charged_rows, ghost_rows[position], axis=0)  10.8 us
  transfers between devices with their start and end apart: 6, of which 0 were waited for; matrix products, arithmetic and copies ran while one was open for 9% of the time, Pallas kernels for 0%

commit v1 on v0

v1 whole, which is shorter than its diff:
```python
import jax
import jax.numpy as jnp
from jax import lax
from jax.experimental import pallas as pl
from jax.experimental.pallas import tpu as pltpu
from jax.sharding import Mesh, PartitionSpec as P

REACH = 3
COARSE = 64
LANES = 128
WIDE = 256
PAD = 8
TILE = 256
CURVE = ("y", "z", "core")
NT = (((1,), (1,)), ((), ()))
BF16 = jnp.bfloat16
F32 = jnp.float32

VMEM = pl.BlockSpec(memory_space=pltpu.VMEM)
SMEM = pl.BlockSpec(memory_space=pltpu.SMEM)
HBM = pl.BlockSpec(memory_space=pltpu.HBM)


def params(mib):
    return pltpu.CompilerParams(vmem_limit_bytes=mib * 2**20)


def cost(flops, bytes_accessed):
    return pl.CostEstimate(flops=flops, bytes_accessed=bytes_accessed, transcendentals=0)


def passed_along(block, axis, distance):
    devices = range(lax.axis_size(axis))
    route = [(i - distance, i) for i in devices if i - distance in devices]
    return lax.ppermute(block, axis, route)


def split_rows(columns):
    points, n = columns.shape
    first = columns[:LANES].T
    rest = jnp.concatenate([columns[LANES:], jnp.zeros((WIDE - points, n), F32)], axis=0)
    return first, rest.T


def picked_rows(load, count):
    sublane = lax.broadcasted_iota(jnp.int32, (8, LANES), 0)
    past = [sublane >= 2 * k for k in range(4)]
    for group in range(count // 4):
        merged = load(4 * group, 0)
        for k in range(1, 4):
            merged = jnp.where(past[k], load(4 * group + k, k), merged)
        yield group, merged


def local_kernel(
    leaf_hbm, occ_hbm, rows_hbm, code_hbm, group_hbm, m2m_hbm, up_hbm, table_ref, partial_ref, *rest
):
    packets = rest[: 2 * REACH]
    padded, chosen, leaf_ref, occ_ref, rows_ref, code_ref, group_ref, m2m_ref, up_ref, sems = rest[
        2 * REACH :
    ]
    copies = [
        pltpu.make_async_copy(source, target, sems.at[n])
        for n, (source, target) in enumerate(
            [
                (occ_hbm, occ_ref),
                (leaf_hbm, leaf_ref),
                (rows_hbm, rows_ref),
                (code_hbm, code_ref),
                (group_hbm, group_ref),
                (m2m_hbm, m2m_ref),
                (up_hbm, up_ref),
            ]
        )
    ]
    for copy in copies:
        copy.start()
    points, slots = leaf_ref.shape
    parents = code_ref.shape[1]
    ghost = rows_ref.shape[1]
    padded[pl.ds(0, PAD), :] = jnp.zeros((PAD, LANES), F32)
    padded[pl.ds(PAD + 2 * slots, PAD), :] = jnp.zeros((PAD, LANES), F32)
    copies[0].wait()
    copies[1].wait()
    for c in range(0, slots, TILE):
        scale = occ_ref[:, c : c + TILE].astype(F32) * 0.03125
        charged = (leaf_ref[:, c : c + TILE].astype(F32) * scale).astype(BF16).astype(F32)
        first, second = split_rows(charged)
        padded[pl.ds(PAD + 2 * c, TILE, stride=2), :] = first
        padded[pl.ds(PAD + 2 * c + 1, TILE, stride=2), :] = second
        table_ref[pl.ds(c, TILE), :] = first
        table_ref[pl.ds(slots + c, TILE), :] = second
    copies[2].wait()

    def one_offset(q, carry):
        base = pl.multiple_of(q * 2 * ghost, 2 * ghost)
        for group, rows in picked_rows(
            lambda n, k: padded[pl.ds(rows_ref[q, n] * 2 + (PAD - 2 * k), 8), :], ghost
        ):
            chosen[pl.ds(base + 8 * group, 8), :] = rows
        return carry

    lax.fori_loop(0, 2 * REACH, one_offset, 0)
    for q in range(2 * REACH):
        first = chosen[pl.ds(q * 2 * ghost, ghost, stride=2), :].T
        second = chosen[pl.ds(q * 2 * ghost + 1, ghost, stride=2), :].T
        packets[q][...] = jnp.concatenate([first, second[: points - LANES]], axis=0).astype(BF16)
    for copy in copies[3:]:
        copy.wait()
    parent = jnp.zeros((points, parents), F32)
    for k in range(8):
        first = table_ref[pl.ds(k, parents, stride=8), :]
        second = table_ref[pl.ds(slots + k, parents, stride=8), :]
        child = jnp.concatenate([first, second], axis=1).astype(BF16)[:, :points]
        parent += lax.dot_general(m2m_ref[k], child, NT, preferred_element_type=F32)
    parent = parent.astype(BF16).astype(F32)
    code = code_ref[...]
    lifted = jnp.zeros((points, parents), F32)
    for k in range(8):
        mine = jnp.where(code == k, parent, 0.0).astype(BF16)
        lifted += jnp.dot(up_ref[k], mine, preferred_element_type=F32)
    high = lifted.astype(BF16)
    low = (lifted - high.astype(F32)).astype(BF16)
    group = lax.broadcasted_iota(jnp.int32, (2 * COARSE, parents), 0)
    left = jnp.where(group == group_ref[...], 1.0, 0.0).astype(BF16)
    right = jnp.where(group - COARSE == group_ref[...], 1.0, 0.0).astype(BF16)

    def summed(member):
        return lax.dot_general(high, member, NT, preferred_element_type=F32) + lax.dot_general(
            low, member, NT, preferred_element_type=F32
        )

    top = partial_ref.shape[0]
    below = jnp.concatenate(
        [summed(right)[top:], jnp.zeros((2 * top - points, 2 * COARSE), F32)], axis=0
    )
    partial_ref[...] = summed(left)[:top] + below


def prepare_kernel(near_ref, m2l_ref, weight_ref, sum_ref):
    offsets, points, _ = m2l_ref.shape
    sum_ref[...] = jnp.sum(near_ref[...], axis=0)

    def one_operator(r, carry):
        operator = m2l_ref[r].astype(F32)
        wide = jnp.concatenate([operator, jnp.zeros((WIDE - points, points), F32)], axis=0)
        first = wide[:, :LANES].T
        second = jnp.concatenate(
            [wide[:, LANES:], jnp.zeros((WIDE, WIDE - points), F32)], axis=1
        ).T
        base = pl.multiple_of(r * WIDE, WIDE)
        weight_ref[pl.ds(base, LANES), :] = first.astype(BF16)
        weight_ref[pl.ds(base + LANES, LANES), :] = second.astype(BF16)
        return carry

    lax.fori_loop(0, offsets, one_operator, 0)


def far_kernel(index_hbm, table_ref, weight_ref, *rest):
    ghosts, (far_ref, table, index, even, odd, index_sem) = rest[: 2 * REACH], rest[2 * REACH :]
    points, ghost = ghosts[0].shape
    slots = far_ref.shape[0]
    tiles = slots // TILE
    pairs = weight_ref.shape[0] // (2 * WIDE)
    chunks = index_sem.shape[0]
    chunk = index.shape[0] // chunks
    boxes = table.reshape(table.shape[0] // 8, 8, LANES)

    def index_copy(n):
        at = pl.ds(pl.multiple_of(n * chunk, chunk), chunk)
        return pltpu.make_async_copy(index_hbm.at[at], index.at[at], index_sem.at[n])

    for n in range(chunks):
        index_copy(n).start()

    def spread(first_box, first, second):
        for sublane in range(8):
            at = pl.ds(first_box * 8 + sublane, TILE, stride=8)
            table[at, :] = second if sublane % 2 else first

    def own_tile(n, carry):
        at = pl.multiple_of(n * TILE, TILE)
        spread(at, table_ref[pl.ds(at, TILE), :], table_ref[pl.ds(slots + at, TILE), :])
        return carry

    lax.fori_loop(0, tiles, own_tile, 0)
    for q in range(2 * REACH):
        spread(slots + q * ghost, *split_rows(ghosts[q][...].astype(F32)))
    table[pl.ds(8 * (slots + 2 * REACH * ghost), 8), :] = jnp.zeros((8, LANES), F32)
    far_ref[...] = jnp.zeros_like(far_ref)
    index_copy(0).wait()

    def gather(step, block):
        pair = step // tiles
        base = (
            (pair // 4) * (8 * slots)
            + lax.rem(step, tiles) * (8 * TILE)
            + lax.rem(pair, 4) * (2 * LANES)
        )
        for half in range(2):
            for j in range(TILE // LANES):
                spot = base + half * LANES + j * 8 * LANES
                for group, rows in picked_rows(lambda n, k: boxes[index[spot + n]], LANES):
                    block[pl.ds(half * 2 * TILE + j * 2 * LANES + 8 * group, 8), :] = rows

    def multiply(step, block):
        pair = step // tiles
        parts = [
            block[pl.ds(half * 2 * TILE + part, TILE, stride=2), :].astype(BF16)
            for half in range(2)
            for part in range(2)
        ]
        weights = weight_ref[pl.ds(pl.multiple_of(pair * 2 * WIDE, 2 * WIDE), 2 * WIDE), :]
        rows = pl.ds(pl.multiple_of(lax.rem(step, tiles) * TILE, TILE), TILE)
        far_ref[rows, :] += jnp.dot(
            jnp.concatenate(parts, axis=1), weights, preferred_element_type=F32
        )

    steps = pairs * tiles
    per_chunk = steps // chunks // 2
    gather(0, even)

    def two_steps(n, carry):
        @pl.when((lax.rem(n + 1, per_chunk) == 0) & (n + 1 < steps // 2))
        def _():
            index_copy((n + 1) // per_chunk).wait()

        gather(2 * n + 1, odd)
        multiply(2 * n, even)
        gather(jnp.minimum(2 * n + 2, steps - 1), even)
        multiply(2 * n + 1, odd)
        return carry

    lax.fori_loop(0, steps // 2, two_steps, 0)


def downward_kernel(
    coarse_ref, far_ref, occ_ref, code_ref, group_ref, list_ref, m2l_ref, l2l_ref, out_ref, first_ref, second_ref
):
    offsets, points, _ = m2l_ref.shape
    parents = code_ref.shape[1]
    slots = out_ref.shape[1]
    top = coarse_ref.shape[1]
    coarse = jnp.sum(coarse_ref[...], axis=0).astype(BF16)
    wanted = list_ref[...]
    wanted = jnp.where(wanted == COARSE, 4 * COARSE, wanted)
    row = lax.broadcasted_iota(jnp.int32, (2 * COARSE, wanted.shape[1]), 0)
    left = jnp.where(row == wanted, 1.0, 0.0).astype(BF16)
    right = jnp.where(row - COARSE == wanted, 1.0, 0.0).astype(BF16)
    upper = jnp.dot(coarse, left, preferred_element_type=F32)
    lower = jnp.dot(coarse, right, preferred_element_type=F32)
    partners = jnp.concatenate([upper, lower[: points - top]], axis=0).astype(BF16)
    sums = [jnp.zeros((points, 2 * COARSE), F32) for _ in range(2)]
    for r in range(offsets):
        at = (r // 2) * 2 * COARSE
        sums[r % 2] += jnp.dot(
            m2l_ref[r], partners[:, at : at + 2 * COARSE], preferred_element_type=F32
        )
    local = (sums[0][:, :COARSE] + sums[1][:, COARSE:]).astype(BF16)
    member = lax.broadcasted_iota(jnp.int32, (COARSE, parents), 0) == group_ref[...]
    pulled = jnp.dot(local, jnp.where(member, 1.0, 0.0).astype(BF16), preferred_element_type=F32)
    code = code_ref[...]
    parent = jnp.zeros((points, parents), F32)
    for k in range(8):
        mine = jnp.where(code == k, pulled, 0.0).astype(BF16)
        parent += jnp.dot(l2l_ref[k], mine, preferred_element_type=F32)
    parent = parent.astype(BF16).astype(F32)
    first, second = split_rows(parent)
    parent_rows = jnp.concatenate([first, second], axis=1).astype(BF16)[:, :points]
    for k in range(8):
        lowered = lax.dot_general(parent_rows, l2l_ref[k], NT, preferred_element_type=F32)
        lowered = jnp.concatenate([lowered, jnp.zeros((parents, WIDE - points), F32)], axis=1)
        first_ref[pl.ds(k, parents, stride=8), :] = lowered[:, :LANES]
        second_ref[pl.ds(k, parents, stride=8), :] = lowered[:, LANES:]
    for c in range(0, slots, TILE):
        rows = pl.ds(c, TILE)
        first = (far_ref[rows, :LANES] + first_ref[rows, :]).T
        second = (far_ref[rows, LANES:] + second_ref[rows, :]).T
        whole = jnp.concatenate([first, second[: points - LANES]], axis=0)
        live = occ_ref[:, c : c + TILE] > 0
        out_ref[:, c : c + TILE] = jnp.where(live, whole, 0.0).astype(BF16)


def shards(
    leaf_mult,
    occupancy,
    ghost_rows,
    m2l_list,
    par_code,
    coarse_of,
    coarse_list,
    m2m,
    coarse_up,
    m2l,
    l2l,
):
    points, slots = leaf_mult.shape
    parents = slots // 8
    offsets = m2l.shape[0]
    ghost = ghost_rows.shape[1]
    top = 80
    shape = jax.ShapeDtypeStruct
    occ = occupancy.reshape(1, slots)
    code = par_code.reshape(1, parents)
    group = coarse_of.reshape(1, parents)

    table, partial, *packets = pl.pallas_call(
        local_kernel,
        out_shape=[shape((2 * slots, LANES), F32), shape((top, 2 * COARSE), F32)]
        + [shape((points, ghost), BF16)] * (2 * REACH),
        in_specs=[HBM] * 7,
        out_specs=[VMEM] * (2 + 2 * REACH),
        scratch_shapes=[
            pltpu.VMEM((2 * slots + 2 * PAD, LANES), F32),
            pltpu.VMEM((4 * REACH * ghost, LANES), F32),
            pltpu.VMEM(leaf_mult.shape, BF16),
            pltpu.VMEM(occ.shape, jnp.int32),
            pltpu.SMEM(ghost_rows.shape, jnp.int32),
            pltpu.VMEM(code.shape, jnp.int32),
            pltpu.VMEM(group.shape, jnp.int32),
            pltpu.VMEM(m2m.shape, BF16),
            pltpu.VMEM(coarse_up.shape, BF16),
            pltpu.SemaphoreType.DMA((7,)),
        ],
        compiler_params=params(60),
        cost_estimate=cost(10**9, 2**22),
        name="local",
    )(leaf_mult, occ, ghost_rows, code, group, m2m, coarse_up)
    near = lax.all_gather(partial, ("y", "oct"))
    stride_list = [stride for stride in range(-REACH, REACH + 1) if stride != 0]
    ghosts = [passed_along(packets[n], CURVE, stride) for n, stride in enumerate(stride_list)]
    weights, near_sum = pl.pallas_call(
        prepare_kernel,
        out_shape=[shape((offsets * WIDE, WIDE), BF16), shape(partial.shape, F32)],
        in_specs=[VMEM, VMEM],
        out_specs=[VMEM, VMEM],
        compiler_params=params(24),
        cost_estimate=cost(10**9, 2**23),
        name="prepare",
    )(near, m2l)
    everywhere = lax.all_gather(near_sum, ("z", "core"))
    index = m2l_list.reshape(offsets // 8, 8, slots // LANES, LANES)
    index = index.transpose(0, 2, 1, 3).reshape(-1)
    far = pl.pallas_call(
        far_kernel,
        out_shape=shape((slots, WIDE), F32),
        in_specs=[HBM] + [VMEM] * (2 + 2 * REACH),
        out_specs=VMEM,
        scratch_shapes=[
            pltpu.VMEM((8 * (slots + 2 * REACH * ghost + 1), LANES), F32),
            pltpu.SMEM((offsets * slots,), jnp.int32),
            pltpu.VMEM((4 * TILE, LANES), F32),
            pltpu.VMEM((4 * TILE, LANES), F32),
            pltpu.SemaphoreType.DMA((4,)),
        ],
        compiler_params=params(40),
        cost_estimate=cost(4 * 10**10, 2**24),
        name="far",
    )(index, table, weights, *ghosts)
    return pl.pallas_call(
        downward_kernel,
        out_shape=shape((points, slots), BF16),
        in_specs=[VMEM] * 8,
        out_specs=VMEM,
        scratch_shapes=[pltpu.VMEM((slots, LANES), F32)] * 2,
        compiler_params=params(32),
        cost_estimate=cost(10**9, 2**23),
        name="downward",
    )(everywhere, far, occ, code, group, coarse_list.reshape(1, -1), m2l, l2l)


def solution(mesh):
    along, across = mesh.devices.shape
    rows = 4 if along % 32 == 0 else 1
    torus = Mesh(
        mesh.devices.reshape(rows, along // rows // 2, 2, across), ("y", "z", "core", "oct")
    )
    boxes = ("y", "z", "core", "oct")
    placed = (
        P(None, boxes),
        P(boxes),
        P(None, boxes),
        P(None, boxes),
        P(boxes),
        P(boxes),
        P(),
        P(),
        P(),
        P(),
        P(),
    )
    return jax.shard_map(
        shards, mesh=torus, in_specs=placed, out_specs=P(None, boxes), check_vma=False
    )
```

time: 517 us -> 176 us (0.34)
  local copies, waits for them, and re-layouts: 336 us -> 16.2 us
  Pallas kernels: 0 us -> 95.6 us
  blocking collectives: 106 us -> 24.6 us
  matrix products: 31.1 us -> 0 us
  other arithmetic: 16.4 us -> 0 us
  between operations: 0.38 us -> 13.6 us
    gather x19 -> x0, local copies, waits for them, and re-layouts: 322 us -> none  [the longest x12 310 us: group_step(): gathered = jnp.take(source_rows, column, axis=0)]
    psum x1 -> x0, blocking collectives: 106 us -> none  [shards(): coarse_mult = lax.psum(partial_sum, ('curve', 'oct')).astype(jnp.bfloat16)]
    pallas_call x0 -> x4, Pallas kernels: none -> 95.6 us  [the longest x1 81.8 us: shards(): pl.pallas_call(far_kernel, out_shape=shape((slots, WIDE), F32), in_specs=...]
    dot_general x12 -> x0, matrix products: 31.1 us -> none  [the longest x8 26.6 us: group_step(): jnp.einsum('rpq,rbq->pb', operator, gathered, preferred_element_type=jnp....]
    all_gather x0 -> x1, blocking collectives: none -> 24.6 us  [shards(): near = lax.all_gather(partial, ('y', 'oct'))]
    unnamed x25 -> x42, local copies, waits for them, and re-layouts: 6.82 us -> 16.1 us
    select_n x18 -> x0, other arithmetic: 8.56 us -> none  [the longest x12 8.43 us: shards(): jnp.take(charged_rows, ghost_rows[position], axis=0)]
  transfers between devices with their start and end apart: 6 -> 7, of which waited for: 0 -> 0; matrix products, arithmetic and copies ran while one was open for 9% -> 0% of each run, Pallas kernels for 0% -> 49%
where the time goes in v1:
time: 176 us; the launch traced here: 175 us
  Pallas kernels  95.6 us (54%)
  starting transfers between devices  25.2 us (14%)
  blocking collectives  24.6 us (14%)
  local copies, waits for them, and re-layouts  16.2 us (9%)
  between operations  13.6 us (8%)
    pallas_call x1, Pallas kernels, shards(): pl.pallas_call(far_kernel, out_shape=shape((slots, WIDE), F32), in_specs=...  81.8 us
    ppermute x6, starting transfers between devices, passed_along(): return lax.ppermute(block, axis, route)  25.2 us
    all_gather x1, blocking collectives, shards(): near = lax.all_gather(partial, ('y', 'oct'))  24.6 us
    unnamed x42, local copies, waits for them, and re-layouts  16.1 us
    pallas_call x1, Pallas kernels, shards(): pl.pallas_call(local_kernel, out_shape=[shape((2 * slots, LANES), F32), s...  6.06 us
    pallas_call x1, Pallas kernels, shards(): pl.pallas_call(prepare_kernel, out_shape=[shape((offsets * WIDE, WIDE), B...  4.06 us
    pallas_call x1, Pallas kernels, shards(): pl.pallas_call(downward_kernel, out_shape=shape((points, slots), BF16), i...  3.69 us
  transfers between devices with their start and end apart: 7, of which 0 were waited for; matrix products, arithmetic and copies ran while one was open for 0% of the time, Pallas kernels for 49%

profile of v1, /device:TPU:1, one launch (start us, length us, event | category | flops | bytes accessed | tf_op | source)
XLA Modules:
  0.0 175.2 jit_solution(10166002357299513245)
XLA Ops:
  6.5 6.1 %local.1 = (f32[4096,128]{1,0:T(8,128)}, f32[80,128]{1,0:T(8,128)}, bf16[152,256]{1,0:T(8,128)(2,1)}, bf16[152,256]{1,0:T(8,128)(2,1)}, bf16[152,256]{1,0:T(8,12...) custom-call(bf16[152,2048]{1,0:T(8,128)(2,1)} %leaf_hbm.1, ...), custom_call_target="tpu_custom_call" | custom-call | flops 1000000000 | bytes 4194304 | tf_op jit(solution)/shard_map/local/pallas_call | solution.py:307
  12.6 1.3 collective-permute-start
  13.9 1.3 collective-permute-start.1
  15.2 8.8 %collective-permute-start.2 = (bf16[152,256]{1,0:T(8,128)(2,1)}, bf16[152,256]{1,0:T(8,128)(2,1)S(1)}, u32[]{:S(2)}, u32[]{:S(2)}) collective-permute-start(bf16[152,256]{1,0:T(8,128)(2,1)} %get-tuple-element.21), channel_id=1, source_target_pairs={{4,0},{8,4},{12,8},{16,12},{20,16},{24,20},{28,24},{32,28},{36,32}... | collective-permute-start | bytes 233480 | tf_op jit(solution)/shard_map/ppermute | solution.py:35
  24.0 4.2 %collective-permute-start.3 = (bf16[152,256]{1,0:T(8,128)(2,1)}, bf16[152,256]{1,0:T(8,128)(2,1)S(1)}, u32[]{:S(2)}, u32[]{:S(2)}) collective-permute-start(bf16[152,256]{1,0:T(8,128)(2,1)} %get-tuple-element.22), channel_id=1, source_target_pairs={{0,4},{4,8},{8,12},{12,16},{16,20},{20,24},{24,28},{28,32},{32,36}... | collective-permute-start | bytes 233480 | tf_op jit(solution)/shard_map/ppermute | solution.py:35
  28.2 4.0 %collective-permute-start.4 = (bf16[152,256]{1,0:T(8,128)(2,1)}, bf16[152,256]{1,0:T(8,128)(2,1)S(1)}, u32[]{:S(2)}, u32[]{:S(2)}) collective-permute-start(bf16[152,256]{1,0:T(8,128)(2,1)} %get-tuple-element.23), channel_id=1, source_target_pairs={{0,8},{4,12},{8,16},{12,20},{16,24},{20,28},{24,32},{28,36},{32,40... | collective-permute-start | bytes 233480 | tf_op jit(solution)/shard_map/ppermute | solution.py:35
  32.2 24.6 %all-gather = f32[1280,128]{1,0:T(8,128)S(1)} all-gather(f32[80,128]{1,0:T(8,128)} %get-tuple-element.15), channel_id=2, replica_groups=mesh['y'=4,'z'=16,'core'=2,'oct'=4] {'y','oct'}, dimensions={0}, use_global_device_ids=true | all-gather | bytes 696320 | tf_op jit(solution)/shard_map/all_gather | solution.py:329
  56.8 5.6 %collective-permute-start.5 = (bf16[152,256]{1,0:T(8,128)(2,1)}, bf16[152,256]{1,0:T(8,128)(2,1)S(1)}, u32[]{:S(2)}, u32[]{:S(2)}) collective-permute-start(bf16[152,256]{1,0:T(8,128)(2,1)} %get-tuple-element.24), channel_id=1, source_target_pairs={{0,12},{4,16},{8,20},{12,24},{16,28},{20,32},{24,36},{28,40},{32,4... | collective-permute-start | bytes 233480 | tf_op jit(solution)/shard_map/ppermute | solution.py:35
  62.5 4.1 %prepare.1 = (bf16[8192,256]{1,0:T(8,128)(2,1)S(1)}, f32[80,128]{1,0:T(8,128)}) custom-call(f32[16,80,128]{2,1,0:T(8,128)S(1)} %bitcast.11, bf16[32,152,152]{2,1,0:T(8,128)(2,1)S(1)} %copy-done), custom_call_target="tpu_custom_call" | custom-call | flops 1000000000 | bytes 8388608 | tf_op jit(solution)/shard_map/prepare/pallas_call | solution.py:332
  66.6 2.0 %copy-done.17 = bf16[8192,256]{1,0:T(8,128)(2,1)} copy-done((bf16[8192,256]{1,0:T(8,128)(2,1)}, bf16[8192,256]{1,0:T(8,128)(2,1)S(1)}, u32[]{:S(2)}) %copy-start.17) | copy-done | bytes 4194328
  69.3 0.6 copy-done.11
  69.9 0.6 copy-done.13
  70.6 0.6 copy-done.15
  71.2 0.9 copy-done.10
  72.1 0.9 copy-done.12
  73.0 0.9 copy-done.14
  73.9 0.9 copy-done.16
  74.7 2.2 %copy-done.18 = bf16[8192,256]{1,0:T(8,128)(2,1)S(1)} copy-done((bf16[8192,256]{1,0:T(8,128)(2,1)S(1)}, bf16[8192,256]{1,0:T(8,128)(2,1)}, u32[]{:S(2)}) %copy-start.18) | copy-done | bytes 4194328
  76.9 1.6 copy-done.19
  78.5 81.8 %far.1.far_ref = f32[2048,256]{1,0:T(8,128)S(1)} custom-call(s32[65536]{0:T(1024)S(1)} %bitcast.18, f32[4096,128]{1,0:T(8,128)S(1)} %copy-done.19, bf16[8192,256]{1,0:T(8,128)(2,1)S(1)} %copy-done.18, bf16[152,256]{1,0:T(8,128)(2,1)S(1)} %collective-permute-done.rest_0_, bf16[152,256]{1,0:T(8,128)(2,1)S(1)} %collective-permute-done.1.rest_1_, ...), custom_call_target="tpu_custom_call" | custom-call | flops 40000000000 | bytes 16777216 | tf_op jit(solution)/shard_map/far/pallas_call | solution.py:344
  160.3 1.3 copy-done.1
  161.7 1.6 copy-done.2
  163.3 1.3 copy-done.3
  164.6 3.7 %downward.1 = bf16[152,2048]{1,0:T(8,128)(2,1)} custom-call(f32[32,80,128]{2,1,0:T(8,128)S(1)} %bitcast.10, f32[2048,256]{1,0:T(8,128)S(1)} %copy-done.2, s32[1,2048]{1,0:T(1,128)S(1)} %bitcast.13, s32[1,256]{1,0:T(1,128)S(1)} %bitcast.15, s32[1,256]{1,0:T(1,128)S(1)} %bitcast.17, s32[1,2048]{1,0:T(1,128)S(1)} %reshape.23.list_ref, ...), custom_call_target="tpu_custom_call" | custom-call | flops 1000000000 | bytes 8388608 | tf_op jit(solution)/shard_map/downward/pallas_call | solution.py:360
  (39 shorter events, 0.8 us)
Async XLA Ops:
  6.5 155.2 %all-gather.4.cloned.1.call-start = ((), (), s32[]{:S(2)}) async-start(), calls=%async_computation | async-start | bytes 1351680 | tf_op jit(solution)/shard_map/all_gather | solution.py:341
  6.5 55.9 %copy-start = (bf16[32,152,152]{2,1,0:T(8,128)(2,1)S(1)}, bf16[32,152,152]{2,1,0:T(8,128)(2,1)}, u32[]{:S(2)}) copy-start(bf16[32,152,152]{2,1,0:T(8,128)(2,1)} %m2l_ref.3) | copy-start | bytes 4435972
  12.6 44.2 %collective-permute-start = (bf16[152,256]{1,0:T(8,128)(2,1)}, bf16[152,256]{1,0:T(8,128)(2,1)S(1)}, u32[]{:S(2)}, u32[]{:S(2)}) collective-permute-start(bf16[152,256]{1,0:T(8,128)(2,1)} %get-tuple-element.19), channel_id=1, source_target_pairs={{12,0},{16,4},{20,8},{24,12},{28,16},{32,20},{36,24},{40,28},{44,3... | collective-permute-start | bytes 233480 | tf_op jit(solution)/shard_map/ppermute | solution.py:35
  13.9 54.7 %collective-permute-start.1 = (bf16[152,256]{1,0:T(8,128)(2,1)}, bf16[152,256]{1,0:T(8,128)(2,1)S(1)}, u32[]{:S(2)}, u32[]{:S(2)}) collective-permute-start(bf16[152,256]{1,0:T(8,128)(2,1)} %get-tuple-element.20), channel_id=1, source_target_pairs={{8,0},{12,4},{16,8},{20,12},{24,16},{28,20},{32,24},{36,28},{40,32... | collective-permute-start | bytes 233480 | tf_op jit(solution)/shard_map/ppermute | solution.py:35
  15.2 53.4 %collective-permute-start.2 = (bf16[152,256]{1,0:T(8,128)(2,1)}, bf16[152,256]{1,0:T(8,128)(2,1)S(1)}, u32[]{:S(2)}, u32[]{:S(2)}) collective-permute-start(bf16[152,256]{1,0:T(8,128)(2,1)} %get-tuple-element.21), channel_id=1, source_target_pairs={{4,0},{8,4},{12,8},{16,12},{20,16},{24,20},{28,24},{32,28},{36,32}... | collective-permute-start | bytes 233480 | tf_op jit(solution)/shard_map/ppermute | solution.py:35
  24.0 45.3 %collective-permute-start.3 = (bf16[152,256]{1,0:T(8,128)(2,1)}, bf16[152,256]{1,0:T(8,128)(2,1)S(1)}, u32[]{:S(2)}, u32[]{:S(2)}) collective-permute-start(bf16[152,256]{1,0:T(8,128)(2,1)} %get-tuple-element.22), channel_id=1, source_target_pairs={{0,4},{4,8},{8,12},{12,16},{16,20},{20,24},{24,28},{28,32},{32,36}... | collective-permute-start | bytes 233480 | tf_op jit(solution)/shard_map/ppermute | solution.py:35
  28.2 41.7 %collective-permute-start.4 = (bf16[152,256]{1,0:T(8,128)(2,1)}, bf16[152,256]{1,0:T(8,128)(2,1)S(1)}, u32[]{:S(2)}, u32[]{:S(2)}) collective-permute-start(bf16[152,256]{1,0:T(8,128)(2,1)} %get-tuple-element.23), channel_id=1, source_target_pairs={{0,8},{4,12},{8,16},{12,20},{16,24},{20,28},{24,32},{28,36},{32,40... | collective-permute-start | bytes 233480 | tf_op jit(solution)/shard_map/ppermute | solution.py:35
  32.2 36.4 %copy-start.20 = (s32[32,64]{1,0:T(8,128)S(1)}, s32[32,64]{1,0:T(8,128)}, u32[]{:S(2)}) copy-start(s32[32,64]{1,0:T(8,128)} %param.17) | copy-start | bytes 24580
  32.2 39.0 %copy-start.8 = (s32[32,2048]{1,0:T(8,128)S(1)}, s32[32,2048]{1,0:T(8,128)}, u32[]{:S(2)}) copy-start(s32[32,2048]{1,0:T(8,128)} %param.14) | copy-start | bytes 786436
  56.8 13.7 %collective-permute-start.5 = (bf16[152,256]{1,0:T(8,128)(2,1)}, bf16[152,256]{1,0:T(8,128)(2,1)S(1)}, u32[]{:S(2)}, u32[]{:S(2)}) collective-permute-start(bf16[152,256]{1,0:T(8,128)(2,1)} %get-tuple-element.24), channel_id=1, source_target_pairs={{0,12},{4,16},{8,20},{12,24},{16,28},{20,32},{24,36},{28,40},{32,4... | collective-permute-start | bytes 233480 | tf_op jit(solution)/shard_map/ppermute | solution.py:35
  66.6 2.0 %copy-start.17 = (bf16[8192,256]{1,0:T(8,128)(2,1)}, bf16[8192,256]{1,0:T(8,128)(2,1)S(1)}, u32[]{:S(2)}) copy-start(bf16[8192,256]{1,0:T(8,128)(2,1)S(1)} %get-tuple-element.18.weight_ref) | copy-start | bytes 12582916
  71.2 0.9 copy-start.10
  72.1 0.9 copy-start.12
  73.0 0.9 copy-start.14
  73.9 0.9 copy-start.16
  74.7 2.2 %copy-start.18 = (bf16[8192,256]{1,0:T(8,128)(2,1)S(1)}, bf16[8192,256]{1,0:T(8,128)(2,1)}, u32[]{:S(2)}) copy-start(bf16[8192,256]{1,0:T(8,128)(2,1)} %copy-done.17) | copy-start | bytes 12582916
  76.9 1.6 copy-start.19
  78.5 83.2 %copy-start.4 = (bf16[8,152,152]{2,1,0:T(8,128)(2,1)S(1)}, bf16[8,152,152]{2,1,0:T(8,128)(2,1)}, u32[]{:S(2)}) copy-start(bf16[8,152,152]{2,1,0:T(8,128)(2,1)} %l2l_ref.1) | copy-start | bytes 1108996
  78.5 83.2 %copy-start.5 = (s32[2048]{0:T(1024)S(1)}, s32[2048]{0:T(1024)}, u32[]{:S(2)}) copy-start(s32[2048]{0:T(1024)} %param.12) | copy-start | bytes 24580
  78.5 83.2 %copy-start.6 = (s32[256]{0:T(256)S(1)}, s32[256]{0:T(256)}, u32[]{:S(2)}) copy-start(s32[256]{0:T(256)} %param.15) | copy-start | bytes 3076
  78.5 83.2 %copy-start.7 = (s32[256]{0:T(256)S(1)}, s32[256]{0:T(256)}, u32[]{:S(2)}) copy-start(s32[256]{0:T(256)} %param.16) | copy-start | bytes 3076
  160.3 1.3 copy-start.1
  161.7 1.6 copy-start.2
  163.3 1.3 copy-start.3
  (4 other events, 2.5 us)
Sparse Core Ops, SparseCore 0:
  68.7 66.6 all-gather.3

commit v2 on v1

v2 whole, which is shorter than its diff:
```python
import jax
import jax.numpy as jnp
from jax import lax
from jax.experimental import pallas as pl
from jax.experimental.pallas import tpu as pltpu
from jax.sharding import Mesh, PartitionSpec as P

REACH = 3
COARSE = 64
LANES = 128
WIDE = 256
PAD = 8
TILE = 256
DEPTH = 2
PART = 80
FAR_MIB = 40
NEAR = ("y", "oct")
OTHER = ("z", "core")
CURVE = ("y", "z", "core")
NT = (((1,), (1,)), ((), ()))
BF16 = jnp.bfloat16
F32 = jnp.float32

VMEM = pl.BlockSpec(memory_space=pltpu.VMEM)
SMEM = pl.BlockSpec(memory_space=pltpu.SMEM)
HBM = pl.BlockSpec(memory_space=pltpu.HBM)


def params(mib):
    return pltpu.CompilerParams(vmem_limit_bytes=mib * 2**20)


def cost(flops, bytes_accessed):
    return pl.CostEstimate(flops=flops, bytes_accessed=bytes_accessed, transcendentals=0)


def passed_along(block, axis, distance):
    devices = range(lax.axis_size(axis))
    route = [(i - distance, i) for i in devices if i - distance in devices]
    return lax.ppermute(block, axis, route)


def split_rows(columns):
    points, n = columns.shape
    first = columns[:LANES].T
    rest = jnp.concatenate([columns[LANES:], jnp.zeros((WIDE - points, n), F32)], axis=0)
    return first, rest.T


def picked_rows(load, count):
    sublane = lax.broadcasted_iota(jnp.int32, (8, LANES), 0)
    past = [sublane >= 2 * k for k in range(4)]
    for group in range(count // 4):
        merged = load(4 * group, 0)
        for k in range(1, 4):
            merged = jnp.where(past[k], load(4 * group + k, k), merged)
        yield group, merged


def local_kernel(
    leaf_hbm, occ_hbm, rows_hbm, code_hbm, group_hbm, m2m_hbm, up_hbm, table_hbm, partial_ref, *rest
):
    packets = rest[: 2 * REACH]
    table_ref, table_sem, padded, chosen, leaf_ref, occ_ref, rows_ref, code_ref, group_ref, m2m_ref, up_ref, sems = rest[
        2 * REACH :
    ]
    copies = [
        pltpu.make_async_copy(source, target, sems.at[n])
        for n, (source, target) in enumerate(
            [
                (occ_hbm, occ_ref),
                (leaf_hbm, leaf_ref),
                (rows_hbm, rows_ref),
                (code_hbm, code_ref),
                (group_hbm, group_ref),
                (m2m_hbm, m2m_ref),
                (up_hbm, up_ref),
            ]
        )
    ]
    for copy in copies:
        copy.start()
    points, slots = leaf_ref.shape
    parents = code_ref.shape[1]
    ghost = rows_ref.shape[1]
    padded[pl.ds(0, PAD), :] = jnp.zeros((PAD, LANES), F32)
    padded[pl.ds(PAD + 2 * slots, PAD), :] = jnp.zeros((PAD, LANES), F32)
    copies[0].wait()
    copies[1].wait()
    for c in range(0, slots, TILE):
        scale = occ_ref[:, c : c + TILE].astype(F32) * 0.03125
        charged = (leaf_ref[:, c : c + TILE].astype(F32) * scale).astype(BF16).astype(F32)
        first, second = split_rows(charged)
        padded[pl.ds(PAD + 2 * c, TILE, stride=2), :] = first
        padded[pl.ds(PAD + 2 * c + 1, TILE, stride=2), :] = second
        table_ref[pl.ds(c, TILE), :] = first
        table_ref[pl.ds(slots + c, TILE), :] = second
    table_copy = pltpu.make_async_copy(table_ref, table_hbm, table_sem)
    table_copy.start()
    copies[2].wait()

    def one_offset(q, carry):
        base = pl.multiple_of(q * 2 * ghost, 2 * ghost)
        for group, rows in picked_rows(
            lambda n, k: padded[pl.ds(rows_ref[q, n] * 2 + (PAD - 2 * k), 8), :], ghost
        ):
            chosen[pl.ds(base + 8 * group, 8), :] = rows
        return carry

    lax.fori_loop(0, 2 * REACH, one_offset, 0)
    for q in range(2 * REACH):
        first = chosen[pl.ds(q * 2 * ghost, ghost, stride=2), :].T
        second = chosen[pl.ds(q * 2 * ghost + 1, ghost, stride=2), :].T
        packets[q][...] = jnp.concatenate([first, second[: points - LANES]], axis=0).astype(BF16)
    for copy in copies[3:]:
        copy.wait()
    parent = jnp.zeros((points, parents), F32)
    for k in range(8):
        first = table_ref[pl.ds(k, parents, stride=8), :]
        second = table_ref[pl.ds(slots + k, parents, stride=8), :]
        child = jnp.concatenate([first, second], axis=1).astype(BF16)[:, :points]
        parent += lax.dot_general(m2m_ref[k], child, NT, preferred_element_type=F32)
    parent = parent.astype(BF16).astype(F32)
    code = code_ref[...]
    lifted = jnp.zeros((points, parents), F32)
    for k in range(8):
        mine = jnp.where(code == k, parent, 0.0).astype(BF16)
        lifted += jnp.dot(up_ref[k], mine, preferred_element_type=F32)
    high = lifted.astype(BF16)
    low = (lifted - high.astype(F32)).astype(BF16)
    group = lax.broadcasted_iota(jnp.int32, (2 * COARSE, parents), 0)
    left = jnp.where(group == group_ref[...], 1.0, 0.0).astype(BF16)
    right = jnp.where(group - COARSE == group_ref[...], 1.0, 0.0).astype(BF16)

    def summed(member):
        return lax.dot_general(high, member, NT, preferred_element_type=F32) + lax.dot_general(
            low, member, NT, preferred_element_type=F32
        )

    top = PART
    below = jnp.concatenate(
        [summed(right)[top:], jnp.zeros((2 * top - points, 2 * COARSE), F32)], axis=0
    )
    partial = summed(left)[:top] + below
    for n in range(partial_ref.shape[0]):
        partial_ref[n] = partial
    table_copy.wait()


def near_kernel(parts_ref, sum_ref):
    sum_ref[...] = jnp.sum(parts_ref[...], axis=0)


def down_kernel(*refs):
    sources, out_ref, targets, (lowered_ref, sems) = refs[:8], refs[8], refs[9:17], refs[17:]
    coarse_ref, list_ref, m2l_ref, group_ref, code_ref, l2l_ref, far_ref, occ_ref = targets
    copies = [
        pltpu.make_async_copy(source, target, sems.at[n])
        for n, (source, target) in enumerate(zip(sources, targets))
    ]
    for copy in copies:
        copy.start()
    for copy in copies:
        copy.wait()
    offsets, points, _ = m2l_ref.shape
    parents = code_ref.shape[1]
    slots = out_ref.shape[1]
    coarse = jnp.sum(coarse_ref[...], axis=0).astype(BF16)
    wanted = list_ref[...]
    wanted = jnp.where(wanted == COARSE, 4 * COARSE, wanted)
    row = lax.broadcasted_iota(jnp.int32, (2 * COARSE, wanted.shape[1]), 0)
    left = jnp.where(row == wanted, 1.0, 0.0).astype(BF16)
    right = jnp.where(row - COARSE == wanted, 1.0, 0.0).astype(BF16)
    upper = jnp.dot(coarse, left, preferred_element_type=F32)
    lower = jnp.dot(coarse, right, preferred_element_type=F32)
    partners = jnp.concatenate([upper, lower[: points - PART]], axis=0).astype(BF16)
    sums = [jnp.zeros((points, 2 * COARSE), F32) for _ in range(2)]
    for r in range(offsets):
        at = (r // 2) * 2 * COARSE
        sums[r % 2] += jnp.dot(
            m2l_ref[r], partners[:, at : at + 2 * COARSE], preferred_element_type=F32
        )
    local = (sums[0][:, :COARSE] + sums[1][:, COARSE:]).astype(BF16)
    member = lax.broadcasted_iota(jnp.int32, (COARSE, parents), 0) == group_ref[...]
    pulled = jnp.dot(local, jnp.where(member, 1.0, 0.0).astype(BF16), preferred_element_type=F32)
    code = code_ref[...]
    parent = jnp.zeros((points, parents), F32)
    for k in range(8):
        mine = jnp.where(code == k, pulled, 0.0).astype(BF16)
        parent += jnp.dot(l2l_ref[k], mine, preferred_element_type=F32)
    parent = parent.astype(BF16).astype(F32)
    first, second = split_rows(parent)
    parent_rows = jnp.concatenate([first, second], axis=1).astype(BF16)[:, :points]
    for k in range(8):
        lowered = lax.dot_general(parent_rows, l2l_ref[k], NT, preferred_element_type=F32)
        lowered = jnp.concatenate([lowered, jnp.zeros((parents, WIDE - points), F32)], axis=1)
        lowered_ref[pl.ds(k, parents, stride=8), :] = lowered[:, :LANES]
        lowered_ref[pl.ds(8 * parents + k, parents, stride=8), :] = lowered[:, LANES:]

    def whole(at):
        rows = pl.ds(at, TILE)
        return (far_ref[rows, :] + lowered_ref[rows, :]).T

    for c in range(0, slots, TILE):
        both = jnp.concatenate([whole(c), whole(slots + c)[: points - LANES]], axis=0)
        live = occ_ref[:, c : c + TILE] > 0
        out_ref[:, c : c + TILE] = jnp.where(live, both, 0.0).astype(BF16)


def parity_split(rows):
    rows = rows.astype(BF16)
    even = lax.rem(lax.broadcasted_iota(jnp.int32, rows.shape, 0), 2) == 0
    zero = jnp.zeros((), BF16)
    return jnp.concatenate([jnp.where(even, rows, zero), jnp.where(even, zero, rows)], axis=1)


def gather_and_translate(accs, windows, window_sems, index, table, m2l_ref, totals):
    points = m2l_ref.shape[1]
    tiles = totals[0].shape[0] // (2 * TILE)
    steps = (m2l_ref.shape[0] // 2) * tiles // 2

    def window_copy(step, slot):
        rows = pl.ds(pl.multiple_of(step * 8, 8), 8)
        return pltpu.make_async_copy(index.at[rows], windows[slot], window_sems.at[slot])

    def load_operators(pair):
        for half in range(2):
            operator = m2l_ref[2 * pair + half].astype(F32)
            operator = jnp.concatenate([operator, jnp.zeros((WIDE - points, points), F32)], axis=0)
            operator = jnp.concatenate([operator, jnp.zeros((WIDE, WIDE - points), F32)], axis=1)
            pltpu.matmul_push_rhs(operator.astype(BF16), 0, half, transpose=True)
            blank = jnp.zeros((2 * TILE, WIDE), BF16)
            pltpu.matmul_acc_lhs(accs[0][half], blank, load_staged_rhs=0)
            totals[1][pl.ds(0, 2 * TILE), :] += pltpu.matmul_pop(accs[0][half])[:, LANES:]

    def gather(slot, which):
        window = windows[slot]

        def load(n, k):
            start = pl.multiple_of(window[4 * which + n // LANES, n % LANES], 8)
            return table[pl.ds(start, 8), :]

        merged = [rows for _, rows in picked_rows(load, 2 * TILE)]
        half = len(merged) // 2
        for n in range(2):
            rows = jnp.concatenate(merged[n * half : (n + 1) * half], axis=0)
            pltpu.matmul_acc_lhs(accs[which][n], parity_split(rows))

    def collect(tile, which):
        rows = pl.ds(pl.multiple_of(lax.rem(tile, tiles) * 2 * TILE, 2 * TILE), 2 * TILE)
        both = pltpu.matmul_pop(accs[which][0]) + pltpu.matmul_pop(accs[which][1])
        totals[0][rows, :] += both[:, :LANES]
        totals[1][rows, :] += both[:, LANES:]

    for slot in range(DEPTH):
        window_copy(slot, slot).start()
    load_operators(0)
    for half in range(2):
        pltpu.matmul_acc_lhs(accs[1][half], jnp.zeros((2 * TILE, WIDE), BF16))

    def some_steps(n, carry):
        for slot in range(DEPTH):
            step = n * DEPTH + slot
            if slot == 0:

                @pl.when((lax.rem(2 * step, tiles) == 0) & (step > 0))
                def _():
                    load_operators(2 * step // tiles)

            window_copy(step, slot).wait()
            gather(slot, 0)
            collect(jnp.maximum(2 * step - 1, 0), 1)
            gather(slot, 1)
            collect(2 * step, 0)
            window_copy(jnp.minimum(step + DEPTH, steps - 1), slot).start()
        return carry

    lax.fori_loop(0, steps // DEPTH, some_steps, 0)
    collect(2 * steps - 1, 1)
    for slot in range(DEPTH):
        window_copy(steps - 1, slot).wait()


def far_kernel(*refs):
    count = 3 + 2 * REACH
    sources, out_ref, targets = refs[:count], refs[count], refs[count + 1 : 2 * count + 1]
    table, index, total_a, total_b, *rest = refs[2 * count + 1 :]
    windows, (sems, window_sems) = rest[:DEPTH], rest[DEPTH:]
    lists, halves, *ghosts = targets[: 2 + 2 * REACH]
    (m2l_ref,) = targets[2 + 2 * REACH :]
    copies = [
        pltpu.make_async_copy(source, target, sems.at[n])
        for n, (source, target) in enumerate(zip(sources, targets))
    ]
    for copy in copies:
        copy.start()
    offsets, points, _ = m2l_ref.shape
    ghost = ghosts[0].shape[1]
    slots = out_ref.shape[0] // 2
    tiles = slots // TILE

    def spread(first_box, first, second):
        for sublane in range(8):
            at = pl.ds(first_box * 8 + sublane, TILE, stride=8)
            table[at, :] = second if sublane % 2 else first

    total_a[...] = jnp.zeros_like(total_a)
    total_b[...] = jnp.zeros_like(total_b)
    table[pl.ds(8 * (slots + 2 * REACH * ghost), 8), :] = jnp.zeros((8, LANES), F32)
    copies[0].wait()
    blocks = TILE // LANES

    def one_tile(bt, carry):
        for r in range(offsets):
            for j in range(blocks):
                column = pl.multiple_of(bt * TILE + j * LANES, LANES)
                row = (((r // 2) * tiles + bt) * 2 + r % 2) * blocks + j
                index[pl.ds(row, 1), :] = lists[r : r + 1, pl.ds(column, LANES)] * 8
        return carry

    lax.fori_loop(0, tiles, one_tile, 0)
    copies[1].wait()

    def own_tile(n, carry):
        at = pl.multiple_of(n * TILE, TILE)
        spread(at, halves[pl.ds(at, TILE), :], halves[pl.ds(slots + at, TILE), :])
        return carry

    lax.fori_loop(0, tiles, own_tile, 0)
    for q in range(2 * REACH):
        copies[2 + q].wait()
        spread(slots + q * ghost, *split_rows(ghosts[q][...].astype(F32)))
    for copy in copies[2 + 2 * REACH :]:
        copy.wait()
    pl.run_scoped(
        lambda *accs: gather_and_translate(
            (accs[:2], accs[2:]), windows, window_sems, index, table, m2l_ref, (total_a, total_b)
        ),
        *[pltpu.ACC(n % 2)((2 * TILE, WIDE), F32) for n in range(4)],
    )

    for n, total in enumerate((total_a, total_b)):
        even, odd = (total[pl.ds(part, slots, stride=2), :] for part in range(2))
        out_ref[pl.ds(n * slots, slots), :] = even + odd


def shards(
    leaf_mult,
    occupancy,
    ghost_rows,
    m2l_list,
    par_code,
    coarse_of,
    coarse_list,
    m2m,
    coarse_up,
    m2l,
    l2l,
):
    points, slots = leaf_mult.shape
    parents = slots // 8
    offsets = m2l.shape[0]
    ghost = ghost_rows.shape[1]
    shape = jax.ShapeDtypeStruct
    occ = occupancy.reshape(1, slots)
    code = par_code.reshape(1, parents)
    group_of = coarse_of.reshape(1, parents)

    near_devices = lax.axis_size(NEAR)
    table, partial, *packets = pl.pallas_call(
        local_kernel,
        out_shape=[shape((2 * slots, LANES), F32), shape((near_devices, PART, 2 * COARSE), F32)]
        + [shape((points, ghost), BF16)] * (2 * REACH),
        in_specs=[HBM] * 7,
        out_specs=[HBM] + [VMEM] * (1 + 2 * REACH),
        scratch_shapes=[
            pltpu.VMEM((2 * slots, LANES), F32),
            pltpu.SemaphoreType.DMA,
            pltpu.VMEM((2 * slots + 2 * PAD, LANES), F32),
            pltpu.VMEM((4 * REACH * ghost, LANES), F32),
            pltpu.VMEM(leaf_mult.shape, BF16),
            pltpu.VMEM(occ.shape, jnp.int32),
            pltpu.SMEM(ghost_rows.shape, jnp.int32),
            pltpu.VMEM(code.shape, jnp.int32),
            pltpu.VMEM(group_of.shape, jnp.int32),
            pltpu.VMEM(m2m.shape, BF16),
            pltpu.VMEM(coarse_up.shape, BF16),
            pltpu.SemaphoreType.DMA((7,)),
        ],
        compiler_params=params(60),
        cost_estimate=cost(10**9, 2**22),
        name="local",
    )(leaf_mult, occ, ghost_rows, code, group_of, m2m, coarse_up)
    near = lax.all_to_all(partial, NEAR, 0, 0, tiled=True)
    near = pl.pallas_call(
        near_kernel,
        out_shape=shape(near.shape[1:], F32),
        in_specs=[VMEM],
        out_specs=VMEM,
        compiler_params=params(8),
        cost_estimate=cost(10**6, 2**18),
        name="near",
    )(near)
    everywhere = lax.all_gather(near, OTHER)
    packets, near = lax.optimization_barrier((packets, near))
    stride_list = [stride for stride in range(-REACH, REACH + 1) if stride != 0]
    ghosts = [passed_along(packets[n], CURVE, stride) for n, stride in enumerate(stride_list)]
    sources = (m2l_list, table, *ghosts, m2l)
    far = pl.pallas_call(
        far_kernel,
        out_shape=shape((2 * slots, LANES), F32),
        in_specs=[HBM] * len(sources),
        out_specs=VMEM,
        scratch_shapes=[pltpu.VMEM(source.shape, source.dtype) for source in sources]
        + [
            pltpu.VMEM((8 * (slots + 2 * REACH * ghost + 1), LANES), F32),
            pltpu.VMEM((offsets * slots // LANES, LANES), jnp.int32),
            pltpu.VMEM((2 * slots, LANES), F32),
            pltpu.VMEM((2 * slots, LANES), F32),
        ]
        + [pltpu.SMEM((4 * TILE // LANES, LANES), jnp.int32)] * DEPTH
        + [
            pltpu.SemaphoreType.DMA((len(sources),)),
            pltpu.SemaphoreType.DMA((DEPTH,)),
        ],
        compiler_params=params(FAR_MIB),
        cost_estimate=cost(10**3, 2**10),
        name="far",
    )(*sources)
    wanted = coarse_list.reshape(1, -1)
    sources = (everywhere, wanted, m2l, group_of, code, l2l, far, occ)
    return pl.pallas_call(
        down_kernel,
        out_shape=shape((points, slots), BF16),
        in_specs=[HBM] * len(sources),
        out_specs=VMEM,
        scratch_shapes=[pltpu.VMEM(source.shape, source.dtype) for source in sources]
        + [pltpu.VMEM((2 * slots, LANES), F32), pltpu.SemaphoreType.DMA((len(sources),))],
        compiler_params=params(24),
        cost_estimate=cost(10**9, 2**23),
        name="down",
    )(*sources)


def solution(mesh):
    along, across = mesh.devices.shape
    rows = 4 if along % 32 == 0 else 1
    torus = Mesh(mesh.devices.reshape(rows, along // rows // 2, 2, across), CURVE + ("oct",))
    boxes = CURVE + ("oct",)
    placed = (
        P(None, boxes),
        P(boxes),
        P(None, boxes),
        P(None, boxes),
        P(boxes),
        P(boxes),
        P(),
        P(),
        P(),
        P(),
        P(),
    )
    return jax.shard_map(
        shards, mesh=torus, in_specs=placed, out_specs=P(None, boxes), check_vma=False
    )
```

time: 176 us -> 139 us (0.79)
  the two profiles are of different devices: /device:TPU:1 before, /device:TPU:9 now
where the time goes in v2:
time: 139 us; the launch traced here: 138 us
  Pallas kernels  62.4 us (45%)
  starting transfers between devices  29.2 us (21%)
  blocking collectives  15.2 us (11%)
  between operations  13.6 us (10%)
  local copies, waits for them, and re-layouts  12 us (9%)
  waiting for transfers between devices  5.75 us (4%)
    pallas_call x1, Pallas kernels, shards(): pl.pallas_call(far_kernel, out_shape=shape((2 * slots, LANES), F32), in_s...  50.9 us
    ppermute x6, starting transfers between devices, passed_along(): return lax.ppermute(block, axis, route)  29.2 us
    all_to_all x1, blocking collectives, shards(): near = lax.all_to_all(partial, NEAR, 0, 0, tiled=True)  15.2 us
    unnamed x38, local copies, waits for them, and re-layouts  11.9 us
    pallas_call x1, Pallas kernels, shards(): pl.pallas_call(local_kernel, out_shape=[shape((2 * slots, LANES), F32), s...  6.41 us
    ppermute x6, waiting for transfers between devices, passed_along(): return lax.ppermute(block, axis, route)  5.73 us
    pallas_call x1, Pallas kernels, shards(): pl.pallas_call(down_kernel, out_shape=shape((points, slots), BF16), in_sp...  4.5 us
  transfers between devices with their start and end apart: 7, of which 2 were waited for; matrix products, arithmetic and copies ran while one was open for 0% of the time, Pallas kernels for 37%

profile of v2, /device:TPU:9, one launch (start us, length us, event | category | flops | bytes accessed | tf_op | source)
XLA Modules:
  0.0 138.0 jit_solution(13184761728330363287)
XLA Ops:
  6.5 6.4 %local.1 = (f32[4096,128]{1,0:T(8,128)}, f32[16,80,128]{2,1,0:T(8,128)}, bf16[152,256]{1,0:T(8,128)(2,1)}, bf16[152,256]{1,0:T(8,128)(2,1)}, bf16[152,256]{1,0:T...) custom-call(bf16[152,2048]{1,0:T(8,128)(2,1)} %leaf_hbm.1, ...), custom_call_target="tpu_custom_call" | custom-call | flops 1000000000 | bytes 4194304 | tf_op jit(solution)/shard_map/local/pallas_call | solution.py:370
  13.0 15.2 %all_to_all.5.parts_ref = f32[16,80,128]{2,1,0:T(8,128)S(1)} all-to-all(f32[16,80,128]{2,1,0:T(8,128)} %get-tuple-element.19), channel_id=1, replica_groups=mesh['y'=4,'z'=16,'core'=2,'oct'=4] {'y','oct'}, dimensions={0} | all-to-all | bytes 1310720 | tf_op jit(solution)/shard_map/all_to_all | solution.py:394
  28.1 0.7 near.1
  28.8 16.4 %collective-permute-start = (bf16[152,256]{1,0:T(8,128)(2,1)}, bf16[152,256]{1,0:T(8,128)(2,1)S(1)}, u32[]{:S(2)}, u32[]{:S(2)}) collective-permute-start(bf16[152,256]{1,0:T(8,128)(2,1)} %get-tuple-element.27), channel_id=1, source_target_pairs={{12,0},{16,4},{20,8},{24,12},{28,16},{32,20},{36,24},{40,28},{44,3... | collective-permute-start | bytes 233480 | tf_op jit(solution)/shard_map/ppermute | solution.py:40
  45.2 2.6 %collective-permute-start.1 = (bf16[152,256]{1,0:T(8,128)(2,1)}, bf16[152,256]{1,0:T(8,128)(2,1)S(1)}, u32[]{:S(2)}, u32[]{:S(2)}) collective-permute-start(bf16[152,256]{1,0:T(8,128)(2,1)} %get-tuple-element.28), channel_id=1, source_target_pairs={{8,0},{12,4},{16,8},{20,12},{24,16},{28,20},{32,24},{36,28},{40,32... | collective-permute-start | bytes 233480 | tf_op jit(solution)/shard_map/ppermute | solution.py:40
  47.8 1.9 %collective-permute-start.2 = (bf16[152,256]{1,0:T(8,128)(2,1)}, bf16[152,256]{1,0:T(8,128)(2,1)S(1)}, u32[]{:S(2)}, u32[]{:S(2)}) collective-permute-start(bf16[152,256]{1,0:T(8,128)(2,1)} %get-tuple-element.29), channel_id=1, source_target_pairs={{4,0},{8,4},{12,8},{16,12},{20,16},{24,20},{28,24},{32,28},{36,32}... | collective-permute-start | bytes 233480 | tf_op jit(solution)/shard_map/ppermute | solution.py:40
  49.8 3.6 %collective-permute-start.3 = (bf16[152,256]{1,0:T(8,128)(2,1)}, bf16[152,256]{1,0:T(8,128)(2,1)S(1)}, u32[]{:S(2)}, u32[]{:S(2)}) collective-permute-start(bf16[152,256]{1,0:T(8,128)(2,1)} %get-tuple-element.30), channel_id=1, source_target_pairs={{0,4},{4,8},{8,12},{12,16},{16,20},{20,24},{24,28},{28,32},{32,36}... | collective-permute-start | bytes 233480 | tf_op jit(solution)/shard_map/ppermute | solution.py:40
  53.4 2.6 %collective-permute-start.4 = (bf16[152,256]{1,0:T(8,128)(2,1)}, bf16[152,256]{1,0:T(8,128)(2,1)S(1)}, u32[]{:S(2)}, u32[]{:S(2)}) collective-permute-start(bf16[152,256]{1,0:T(8,128)(2,1)} %get-tuple-element.31), channel_id=1, source_target_pairs={{0,8},{4,12},{8,16},{12,20},{16,24},{20,28},{24,32},{28,36},{32,40... | collective-permute-start | bytes 233480 | tf_op jit(solution)/shard_map/ppermute | solution.py:40
  56.1 1.9 %collective-permute-start.5 = (bf16[152,256]{1,0:T(8,128)(2,1)}, bf16[152,256]{1,0:T(8,128)(2,1)S(1)}, u32[]{:S(2)}, u32[]{:S(2)}) collective-permute-start(bf16[152,256]{1,0:T(8,128)(2,1)} %get-tuple-element.32), channel_id=1, source_target_pairs={{0,12},{4,16},{8,20},{12,24},{16,28},{20,32},{24,36},{28,40},{32,4... | collective-permute-start | bytes 233480 | tf_op jit(solution)/shard_map/ppermute | solution.py:40
  58.1 0.6 copy-done.7
  58.8 0.6 copy-done.9
  59.4 2.5 %collective-permute-done.4.refs_6_ = bf16[152,256]{1,0:T(8,128)(2,1)S(1)} collective-permute-done((bf16[152,256]{1,0:T(8,128)(2,1)}, bf16[152,256]{1,0:T(8,128)(2,1)S(1)}, u32[]{:S(2)}, u32[]{:S(2)}) %collective-permute-start.4) | collective-permute-done | bytes 77856 | tf_op jit(solution)/shard_map/ppermute | solution.py:40
  62.5 3.2 %collective-permute-done.5.refs_7_ = bf16[152,256]{1,0:T(8,128)(2,1)S(1)} collective-permute-done((bf16[152,256]{1,0:T(8,128)(2,1)}, bf16[152,256]{1,0:T(8,128)(2,1)S(1)}, u32[]{:S(2)}, u32[]{:S(2)}) %collective-permute-start.5) | collective-permute-done | bytes 77856 | tf_op jit(solution)/shard_map/ppermute | solution.py:40
  65.7 0.6 copy-done.13
  66.4 1.6 %copy-done.3 = f32[4096,128]{1,0:T(8,128)S(1)} copy-done((f32[4096,128]{1,0:T(8,128)S(1)}, f32[4096,128]{1,0:T(8,128)}, u32[]{:S(2)}) %copy-start.3) | copy-done | bytes 2097176
  68.0 0.9 copy-done.8
  68.9 0.9 copy-done.10
  69.7 0.9 copy-done.12
  70.6 0.9 copy-done.14
  71.5 50.9 %far.1.refs_6_ = f32[4096,128]{1,0:T(8,128)S(1)} custom-call(s32[32,2048]{1,0:T(8,128)S(1)} %copy-done.6, f32[4096,128]{1,0:T(8,128)S(1)} %copy-done.3, bf16[152,256]{1,0:T(8,128)(2,1)S(1)} %collective-permute-done.refs_2_, bf16[152,256]{1,0:T(8,128)(2,1)S(1)} %collective-permute-done.1.refs_3_, bf16[152,256]{1,0:T(8,128)(2,1)S(1)} %copy-done.8, ...), custom_call_target="tpu_custom_call" | custom-call | flops 1000 | bytes 1024 | tf_op jit(solution)/shard_map/far/pallas_call | solution.py:409
  122.4 1.3 copy-done.1
  123.8 1.6 %copy-done.2 = f32[4096,128]{1,0:T(8,128)S(1)} copy-done((f32[4096,128]{1,0:T(8,128)S(1)}, f32[4096,128]{1,0:T(8,128)}, u32[]{:S(2)}) %copy-start.2) | copy-done | bytes 2097176
  125.4 1.3 copy-done.4
  126.7 4.5 %down.1 = bf16[152,2048]{1,0:T(8,128)(2,1)} custom-call(f32[32,80,128]{2,1,0:T(8,128)S(1)} %bitcast.4, s32[1,2048]{1,0:T(1,128)S(1)} %reshape.15.refs_1_, bf16[32,152,152]{2,1,0:T(8,128)(2,1)S(1)} %copy-done, s32[1,256]{1,0:T(1,128)S(1)} %bitcast.10, s32[1,256]{1,0:T(1,128)S(1)} %bitcast.8, bf16[8,152,152]{2,1,0:T(8,128)(2,1)S(1)} %copy-done.5, ...), custom_call_target="tpu_custom_call" | custom-call | flops 1000000000 | bytes 8388608 | tf_op jit(solution)/shard_map/down/pallas_call | solution.py:432
  (35 shorter events, 0.8 us)
Async XLA Ops:
  6.5 117.2 %all-gather.3.cloned.1.call-start = ((), (), s32[]{:S(2)}) async-start(), calls=%async_computation.1 | async-start | bytes 1351680 | tf_op jit(solution)/shard_map/all_gather | solution.py:404
  6.5 51.5 %copy-start.18 = (s32[32,64]{1,0:T(8,128)S(1)}, s32[32,64]{1,0:T(8,128)}, u32[]{:S(2)}) copy-start(s32[32,64]{1,0:T(8,128)} %param.17) | copy-start | bytes 24580
  6.5 59.8 %copy-start = (bf16[32,152,152]{2,1,0:T(8,128)(2,1)S(1)}, bf16[32,152,152]{2,1,0:T(8,128)(2,1)}, u32[]{:S(2)}) copy-start(bf16[32,152,152]{2,1,0:T(8,128)(2,1)} %refs_2_.1) | copy-start | bytes 4435972
  6.5 59.8 %copy-start.6 = (s32[32,2048]{1,0:T(8,128)S(1)}, s32[32,2048]{1,0:T(8,128)}, u32[]{:S(2)}) copy-start(s32[32,2048]{1,0:T(8,128)} %refs_0_.1) | copy-start | bytes 786436
  28.8 27.3 %collective-permute-start = (bf16[152,256]{1,0:T(8,128)(2,1)}, bf16[152,256]{1,0:T(8,128)(2,1)S(1)}, u32[]{:S(2)}, u32[]{:S(2)}) collective-permute-start(bf16[152,256]{1,0:T(8,128)(2,1)} %get-tuple-element.27), channel_id=1, source_target_pairs={{12,0},{16,4},{20,8},{24,12},{28,16},{32,20},{36,24},{40,28},{44,3... | collective-permute-start | bytes 233480 | tf_op jit(solution)/shard_map/ppermute | solution.py:40
  45.2 12.9 %collective-permute-start.1 = (bf16[152,256]{1,0:T(8,128)(2,1)}, bf16[152,256]{1,0:T(8,128)(2,1)S(1)}, u32[]{:S(2)}, u32[]{:S(2)}) collective-permute-start(bf16[152,256]{1,0:T(8,128)(2,1)} %get-tuple-element.28), channel_id=1, source_target_pairs={{8,0},{12,4},{16,8},{20,12},{24,16},{28,20},{32,24},{36,28},{40,32... | collective-permute-start | bytes 233480 | tf_op jit(solution)/shard_map/ppermute | solution.py:40
  47.8 10.3 %collective-permute-start.2 = (bf16[152,256]{1,0:T(8,128)(2,1)}, bf16[152,256]{1,0:T(8,128)(2,1)S(1)}, u32[]{:S(2)}, u32[]{:S(2)}) collective-permute-start(bf16[152,256]{1,0:T(8,128)(2,1)} %get-tuple-element.29), channel_id=1, source_target_pairs={{4,0},{8,4},{12,8},{16,12},{20,16},{24,20},{28,24},{32,28},{36,32}... | collective-permute-start | bytes 233480 | tf_op jit(solution)/shard_map/ppermute | solution.py:40
  49.8 9.0 %collective-permute-start.3 = (bf16[152,256]{1,0:T(8,128)(2,1)}, bf16[152,256]{1,0:T(8,128)(2,1)S(1)}, u32[]{:S(2)}, u32[]{:S(2)}) collective-permute-start(bf16[152,256]{1,0:T(8,128)(2,1)} %get-tuple-element.30), channel_id=1, source_target_pairs={{0,4},{4,8},{8,12},{12,16},{16,20},{20,24},{24,28},{28,32},{32,36}... | collective-permute-start | bytes 233480 | tf_op jit(solution)/shard_map/ppermute | solution.py:40
  53.4 8.5 %collective-permute-start.4 = (bf16[152,256]{1,0:T(8,128)(2,1)}, bf16[152,256]{1,0:T(8,128)(2,1)S(1)}, u32[]{:S(2)}, u32[]{:S(2)}) collective-permute-start(bf16[152,256]{1,0:T(8,128)(2,1)} %get-tuple-element.31), channel_id=1, source_target_pairs={{0,8},{4,12},{8,16},{12,20},{16,24},{20,28},{24,32},{28,36},{32,40... | collective-permute-start | bytes 233480 | tf_op jit(solution)/shard_map/ppermute | solution.py:40
  56.1 9.7 %collective-permute-start.5 = (bf16[152,256]{1,0:T(8,128)(2,1)}, bf16[152,256]{1,0:T(8,128)(2,1)S(1)}, u32[]{:S(2)}, u32[]{:S(2)}) collective-permute-start(bf16[152,256]{1,0:T(8,128)(2,1)} %get-tuple-element.32), channel_id=1, source_target_pairs={{0,12},{4,16},{8,20},{12,24},{16,28},{20,32},{24,36},{28,40},{32,4... | collective-permute-start | bytes 233480 | tf_op jit(solution)/shard_map/ppermute | solution.py:40
  58.1 0.6 copy-start.7
  58.8 0.6 copy-start.9
  66.4 1.6 %copy-start.3 = (f32[4096,128]{1,0:T(8,128)S(1)}, f32[4096,128]{1,0:T(8,128)}, u32[]{:S(2)}) copy-start(f32[4096,128]{1,0:T(8,128)} %get-tuple-element.20.refs_1_) | copy-start | bytes 6291460
  68.0 0.9 copy-start.8
  68.9 0.9 copy-start.10
  69.7 0.9 copy-start.12
  70.6 0.9 copy-start.14
  71.5 52.2 %copy-start.5 = (bf16[8,152,152]{2,1,0:T(8,128)(2,1)S(1)}, bf16[8,152,152]{2,1,0:T(8,128)(2,1)}, u32[]{:S(2)}) copy-start(bf16[8,152,152]{2,1,0:T(8,128)(2,1)} %refs_5_.1) | copy-start | bytes 1108996
  71.5 52.2 %copy-start.15 = (s32[2048]{0:T(1024)S(1)}, s32[2048]{0:T(1024)}, u32[]{:S(2)}) copy-start(s32[2048]{0:T(1024)} %param.12) | copy-start | bytes 24580
  71.5 52.2 %copy-start.16 = (s32[256]{0:T(256)S(1)}, s32[256]{0:T(256)}, u32[]{:S(2)}) copy-start(s32[256]{0:T(256)} %param.15) | copy-start | bytes 3076
  71.5 52.2 %copy-start.17 = (s32[256]{0:T(256)S(1)}, s32[256]{0:T(256)}, u32[]{:S(2)}) copy-start(s32[256]{0:T(256)} %param.16) | copy-start | bytes 3076
  122.4 1.3 copy-start.1
  123.8 1.6 %copy-start.2 = (f32[4096,128]{1,0:T(8,128)S(1)}, f32[4096,128]{1,0:T(8,128)}, u32[]{:S(2)}) copy-start(f32[4096,128]{1,0:T(8,128)} %copy-done.1) | copy-start | bytes 6291460
  125.4 1.3 copy-start.4
  (2 other events, 1.3 us)
Sparse Core Ops, SparseCore 0:
  28.9 77.0 all-gather.2

commit v3 on v2

--- a/solution.py
+++ b/solution.py
@@ -141,19 +141,32 @@
     below = jnp.concatenate(
         [summed(right)[top:], jnp.zeros((2 * top - points, 2 * COARSE), F32)], axis=0
     )
-    partial = summed(left)[:top] + below
-    for n in range(partial_ref.shape[0]):
-        partial_ref[n] = partial
+    partial_ref[pl.ds(0, top), :] = summed(left)[:top] + below
+    partial_ref[pl.ds(top, LANES - top), :] = jnp.zeros((LANES - top, LANES), F32)
     table_copy.wait()
 
 
 def near_kernel(parts_ref, sum_ref):
-    sum_ref[...] = jnp.sum(parts_ref[...], axis=0)
+    total = jnp.sum(parts_ref[...], axis=0)
+    for n in range(sum_ref.shape[0]):
+        sum_ref[n] = total
+
+
+def summed_parts(parts, copies, name):
+    return pl.pallas_call(
+        near_kernel,
+        out_shape=jax.ShapeDtypeStruct((copies,) + parts.shape[1:], F32),
+        in_specs=[VMEM],
+        out_specs=VMEM,
+        compiler_params=params(8),
+        cost_estimate=cost(10**6, 2**18),
+        name=name,
+    )(parts)
 
 
 def down_kernel(*refs):
-    sources, out_ref, targets, (lowered_ref, sems) = refs[:8], refs[8], refs[9:17], refs[17:]
-    coarse_ref, list_ref, m2l_ref, group_ref, code_ref, l2l_ref, far_ref, occ_ref = targets
+    sources, lowered_ref, targets, sems = refs[:6], refs[6], refs[7:13], refs[13]
+    coarse_ref, list_ref, m2l_ref, group_ref, code_ref, l2l_ref = targets
     copies = [
         pltpu.make_async_copy(source, target, sems.at[n])
         for n, (source, target) in enumerate(zip(sources, targets))
@@ -164,8 +177,7 @@
         copy.wait()
     offsets, points, _ = m2l_ref.shape
     parents = code_ref.shape[1]
-    slots = out_ref.shape[1]
-    coarse = jnp.sum(coarse_ref[...], axis=0).astype(BF16)
+    coarse = coarse_ref[...].reshape(-1, 2 * COARSE)[:PART].astype(BF16)
     wanted = list_ref[...]
     wanted = jnp.where(wanted == COARSE, 4 * COARSE, wanted)
     row = lax.broadcasted_iota(jnp.int32, (2 * COARSE, wanted.shape[1]), 0)
@@ -197,15 +209,6 @@
         lowered_ref[pl.ds(k, parents, stride=8), :] = lowered[:, :LANES]
         lowered_ref[pl.ds(8 * parents + k, parents, stride=8), :] = lowered[:, LANES:]
 
-    def whole(at):
-        rows = pl.ds(at, TILE)
-        return (far_ref[rows, :] + lowered_ref[rows, :]).T
-
-    for c in range(0, slots, TILE):
-        both = jnp.concatenate([whole(c), whole(slots + c)[: points - LANES]], axis=0)
-        live = occ_ref[:, c : c + TILE] > 0
-        out_ref[:, c : c + TILE] = jnp.where(live, both, 0.0).astype(BF16)
-
 
 def parity_split(rows):
     rows = rows.astype(BF16)
@@ -238,7 +241,7 @@
 
         def load(n, k):
             start = pl.multiple_of(window[4 * which + n // LANES, n % LANES], 8)
-            return table[pl.ds(start, 8), :]
+            return pltpu.annotate(table, no_bank_conflict=True)[pl.ds(start, 8), :]
 
         merged = [rows for _, rows in picked_rows(load, 2 * TILE)]
         half = len(merged) // 2
@@ -282,12 +285,12 @@
 
 
 def far_kernel(*refs):
-    count = 3 + 2 * REACH
+    count = 5 + 2 * REACH
     sources, out_ref, targets = refs[:count], refs[count], refs[count + 1 : 2 * count + 1]
     table, index, total_a, total_b, *rest = refs[2 * count + 1 :]
     windows, (sems, window_sems) = rest[:DEPTH], rest[DEPTH:]
     lists, halves, *ghosts = targets[: 2 + 2 * REACH]
-    (m2l_ref,) = targets[2 + 2 * REACH :]
+    m2l_ref, occ_ref, lowered_ref = targets[2 + 2 * REACH :]
     copies = [
         pltpu.make_async_copy(source, target, sems.at[n])
         for n, (source, target) in enumerate(zip(sources, targets))
@@ -296,7 +299,7 @@
         copy.start()
     offsets, points, _ = m2l_ref.shape
     ghost = ghosts[0].shape[1]
-    slots = out_ref.shape[0] // 2
+    slots = out_ref.shape[1]
     tiles = slots // TILE
 
     def spread(first_box, first, second):
@@ -339,9 +342,15 @@
         *[pltpu.ACC(n % 2)((2 * TILE, WIDE), F32) for n in range(4)],
     )
 
-    for n, total in enumerate((total_a, total_b)):
-        even, odd = (total[pl.ds(part, slots, stride=2), :] for part in range(2))
-        out_ref[pl.ds(n * slots, slots), :] = even + odd
+    def whole(total, at, c):
+        even, odd = (total[pl.ds(2 * c + part, TILE, stride=2), :] for part in range(2))
+        return (even + odd + lowered_ref[pl.ds(at + c, TILE), :]).T
+
+    for c in range(0, slots, TILE):
+        second = whole(total_b, slots, c)[: points - LANES]
+        both = jnp.concatenate([whole(total_a, 0, c), second], axis=0)
+        live = occ_ref[:, c : c + TILE] > 0
+        out_ref[:, c : c + TILE] = jnp.where(live, both, 0.0).astype(BF16)
 
 
 def shards(
@@ -369,7 +378,7 @@
     near_devices = lax.axis_size(NEAR)
     table, partial, *packets = pl.pallas_call(
         local_kernel,
-        out_shape=[shape((2 * slots, LANES), F32), shape((near_devices, PART, 2 * COARSE), F32)]
+        out_shape=[shape((2 * slots, LANES), F32), shape((LANES, 2 * COARSE), F32)]
         + [shape((points, ghost), BF16)] * (2 * REACH),
         in_specs=[HBM] * 7,
         out_specs=[HBM] + [VMEM] * (1 + 2 * REACH),
@@ -391,24 +400,30 @@
         cost_estimate=cost(10**9, 2**22),
         name="local",
     )(leaf_mult, occ, ghost_rows, code, group_of, m2m, coarse_up)
-    near = lax.all_to_all(partial, NEAR, 0, 0, tiled=True)
-    near = pl.pallas_call(
-        near_kernel,
-        out_shape=shape(near.shape[1:], F32),
-        in_specs=[VMEM],
-        out_specs=VMEM,
-        compiler_params=params(8),
-        cost_estimate=cost(10**6, 2**18),
-        name="near",
-    )(near)
-    everywhere = lax.all_gather(near, OTHER)
-    packets, near = lax.optimization_barrier((packets, near))
+    slices = partial.reshape(near_devices, LANES // near_devices, 2 * COARSE)
+    for group, following in ((NEAR, OTHER), (OTHER, NEAR)):
+        slices = lax.all_to_all(slices, group, 0, 0, tiled=True)
+        slices = summed_parts(slices, lax.axis_size(following), "sum_over_" + group[0])
     stride_list = [stride for stride in range(-REACH, REACH + 1) if stride != 0]
     ghosts = [passed_along(packets[n], CURVE, stride) for n, stride in enumerate(stride_list)]
-    sources = (m2l_list, table, *ghosts, m2l)
-    far = pl.pallas_call(
+    everywhere = lax.all_to_all(slices, NEAR, 0, 0, tiled=True)
+    wanted = coarse_list.reshape(1, -1)
+    sources = (everywhere, wanted, m2l, group_of, code, l2l)
+    lowered = pl.pallas_call(
+        down_kernel,
+        out_shape=shape((2 * slots, LANES), F32),
+        in_specs=[HBM] * len(sources),
+        out_specs=VMEM,
+        scratch_shapes=[pltpu.VMEM(source.shape, source.dtype) for source in sources]
+        + [pltpu.SemaphoreType.DMA((len(sources),))],
+        compiler_params=params(24),
+        cost_estimate=cost(10**9, 2**23),
+        name="down",
+    )(*sources)
+    sources = (m2l_list, table, *ghosts, m2l, occ, lowered)
+    return pl.pallas_call(
         far_kernel,
-        out_shape=shape((2 * slots, LANES), F32),
+        out_shape=shape((points, slots), BF16),
         in_specs=[HBM] * len(sources),
         out_specs=VMEM,
         scratch_shapes=[pltpu.VMEM(source.shape, source.dtype) for source in sources]
@@ -424,21 +439,8 @@
             pltpu.SemaphoreType.DMA((DEPTH,)),
         ],
         compiler_params=params(FAR_MIB),
-        cost_estimate=cost(10**3, 2**10),
+        cost_estimate=cost(4 * 10**10, 2**24),
         name="far",
-    )(*sources)
-    wanted = coarse_list.reshape(1, -1)
-    sources = (everywhere, wanted, m2l, group_of, code, l2l, far, occ)
-    return pl.pallas_call(
-        down_kernel,
-        out_shape=shape((points, slots), BF16),
-        in_specs=[HBM] * len(sources),
-        out_specs=VMEM,
-        scratch_shapes=[pltpu.VMEM(source.shape, source.dtype) for source in sources]
-        + [pltpu.VMEM((2 * slots, LANES), F32), pltpu.SemaphoreType.DMA((len(sources),))],
-        compiler_params=params(24),
-        cost_estimate=cost(10**9, 2**23),
-        name="down",
     )(*sources)
 
 

time: 139 us -> 132 us (0.950)
  the two profiles are of different devices: /device:TPU:9 before, /device:TPU:10 now
where the time goes in v3:
time: 132 us
  Pallas kernels  62.5 us (47%)
  starting transfers between devices  38.3 us (29%)
  waiting for transfers between devices  15.7 us (12%)
  blocking collectives  14.5 us (11%)
    pallas_call x1, Pallas kernels, shards(): pl.pallas_call(far_kernel, out_shape=shape((points, slots), BF16), in_spe...  51.8 us
    ppermute x6, starting transfers between devices, passed_along(): return lax.ppermute(block, axis, route)  18.9 us
    all_to_all x1, blocking collectives, shards(): slices = lax.all_to_all(slices, group, 0, 0, tiled=True)  14.5 us
    all_to_all x1, starting transfers between devices, shards(): slices = lax.all_to_all(slices, group, 0, 0, tiled=True)  13.7 us
    all_to_all x1, waiting for transfers between devices, shards(): slices = lax.all_to_all(slices, group, 0, 0, tiled=True)  10.6 us
    pallas_call x1, Pallas kernels, shards(): pl.pallas_call(local_kernel, out_shape=[shape((2 * slots, LANES), F32), s...  6.21 us
    all_to_all x1, starting transfers between devices, shards(): everywhere = lax.all_to_all(slices, NEAR, 0, 0, tiled=True)  5.7 us
    ppermute x6, waiting for transfers between devices, passed_along(): return lax.ppermute(block, axis, route)  5.11 us
  transfers between devices with their start and end apart: 8, of which 2 were waited for; matrix products, arithmetic and copies ran while one was open for 0% of the time, Pallas kernels for 3%

profile of v3, /device:TPU:10, one launch (start us, length us, event | category | flops | bytes accessed | tf_op | source)
XLA Modules:
  0.0 132.0 jit_solution(1220192710686927685)
XLA Ops:
  0.0 6.2 %local.1 = (f32[4096,128]{1,0:T(8,128)}, f32[128,128]{1,0:T(8,128)}, bf16[152,256]{1,0:T(8,128)(2,1)}, bf16[152,256]{1,0:T(8,128)(2,1)}, bf16[152,256]{1,0:T(8,1...) custom-call(bf16[152,2048]{1,0:T(8,128)(2,1)} %leaf_hbm.1, ...), custom_call_target="tpu_custom_call" | custom-call | flops 1000000000 | bytes 4194304 | tf_op jit(solution)/shard_map/local/pallas_call | solution.py:379
  6.3 14.5 %all_to_all.15.parts_ref = f32[16,8,128]{2,1,0:T(8,128)S(1)} all-to-all(f32[16,8,128]{2,1,0:T(8,128)} %bitcast.10), channel_id=1, replica_groups=mesh['y'=4,'z'=16,'core'=2,'oct'=4] {'y','oct'}, dimensions={0} | all-to-all | bytes 131072 | tf_op jit(solution)/shard_map/all_to_all | solution.py:405
  20.8 0.7 sum_over_y.1
  21.4 13.7 %all-to-all-start.1 = ((f32[32,8,128]{2,1,0:T(8,128)}), f32[32,8,128]{2,1,0:T(8,128)S(1)}, u32[]{:S(2)}, u32[]{:S(2)}) async-start(f32[32,8,128]{2,1,0:T(8,128)} %sum_over_y.1), calls=%async_computation.1 | async-start | bytes 262144 | tf_op jit(solution)/shard_map/all_to_all | solution.py:405
  35.2 6.6 %collective-permute-start = (bf16[152,256]{1,0:T(8,128)(2,1)}, bf16[152,256]{1,0:T(8,128)(2,1)S(1)}, u32[]{:S(2)}, u32[]{:S(2)}) collective-permute-start(bf16[152,256]{1,0:T(8,128)(2,1)} %get-tuple-element.14), channel_id=1, source_target_pairs={{12,0},{16,4},{20,8},{24,12},{28,16},{32,20},{36,24},{40,28},{44,3... | collective-permute-start | bytes 233480 | tf_op jit(solution)/shard_map/ppermute | solution.py:40
  41.7 10.6 %all-to-all-done.1.parts_ref = f32[32,8,128]{2,1,0:T(8,128)S(1)} async-done(((f32[32,8,128]{2,1,0:T(8,128)}), f32[32,8,128]{2,1,0:T(8,128)S(1)}, u32[]{:S(2)}, u32[]{:S(2)}) %all-to-all-start.1) | async-done | bytes 131104 | tf_op jit(solution)/shard_map/all_to_all | solution.py:405
  52.4 0.7 sum_over_z.1
  53.0 5.7 %all-to-all-start.2 = ((f32[16,8,128]{2,1,0:T(8,128)}), f32[16,8,128]{2,1,0:T(8,128)S(1)}, u32[]{:S(2)}, u32[]{:S(2)}) async-start(f32[16,8,128]{2,1,0:T(8,128)} %sum_over_z.1), calls=%async_computation.2 | async-start | bytes 131072 | tf_op jit(solution)/shard_map/all_to_all | solution.py:409
  58.7 1.9 %collective-permute-start.1 = (bf16[152,256]{1,0:T(8,128)(2,1)}, bf16[152,256]{1,0:T(8,128)(2,1)}, u32[]{:S(2)}, u32[]{:S(2)}) collective-permute-start(bf16[152,256]{1,0:T(8,128)(2,1)} %get-tuple-element.15), channel_id=1, source_target_pairs={{8,0},{12,4},{16,8},{20,12},{24,16},{28,20},{32,24},{36,28},{40,32... | collective-permute-start | bytes 233480 | tf_op jit(solution)/shard_map/ppermute | solution.py:40
  60.7 1.9 %collective-permute-start.2 = (bf16[152,256]{1,0:T(8,128)(2,1)}, bf16[152,256]{1,0:T(8,128)(2,1)}, u32[]{:S(2)}, u32[]{:S(2)}) collective-permute-start(bf16[152,256]{1,0:T(8,128)(2,1)} %get-tuple-element.16), channel_id=1, source_target_pairs={{4,0},{8,4},{12,8},{16,12},{20,16},{24,20},{28,24},{32,28},{36,32}... | collective-permute-start | bytes 233480 | tf_op jit(solution)/shard_map/ppermute | solution.py:40
  62.6 2.4 %collective-permute-start.3 = (bf16[152,256]{1,0:T(8,128)(2,1)}, bf16[152,256]{1,0:T(8,128)(2,1)}, u32[]{:S(2)}, u32[]{:S(2)}) collective-permute-start(bf16[152,256]{1,0:T(8,128)(2,1)} %get-tuple-element.17), channel_id=1, source_target_pairs={{0,4},{4,8},{8,12},{12,16},{16,20},{20,24},{24,28},{28,32},{32,36}... | collective-permute-start | bytes 233480 | tf_op jit(solution)/shard_map/ppermute | solution.py:40
  65.0 3.9 %collective-permute-start.4 = (bf16[152,256]{1,0:T(8,128)(2,1)}, bf16[152,256]{1,0:T(8,128)(2,1)}, u32[]{:S(2)}, u32[]{:S(2)}) collective-permute-start(bf16[152,256]{1,0:T(8,128)(2,1)} %get-tuple-element.18), channel_id=1, source_target_pairs={{0,8},{4,12},{8,16},{12,20},{16,24},{20,28},{24,32},{28,36},{32,40... | collective-permute-start | bytes 233480 | tf_op jit(solution)/shard_map/ppermute | solution.py:40
  68.9 0.1 reshape.19.refs_1_
  69.0 0.0 copy-start.5
  69.0 0.6 copy-done.5
  69.7 2.1 %collective-permute-start.5 = (bf16[152,256]{1,0:T(8,128)(2,1)}, bf16[152,256]{1,0:T(8,128)(2,1)}, u32[]{:S(2)}, u32[]{:S(2)}) collective-permute-start(bf16[152,256]{1,0:T(8,128)(2,1)} %get-tuple-element.19), channel_id=1, source_target_pairs={{0,12},{4,16},{8,20},{12,24},{16,28},{20,32},{24,36},{28,40},{32,4... | collective-permute-start | bytes 233480 | tf_op jit(solution)/shard_map/ppermute | solution.py:40
  71.8 0.0 all-to-all-done.2.refs_0_
  71.9 0.0 copy-start.6
  71.9 3.2 %down.1.refs_10_ = f32[4096,128]{1,0:T(8,128)S(1)} custom-call(f32[16,8,128]{2,1,0:T(8,128)S(1)} %all-to-all-done.2.refs_0_, s32[1,2048]{1,0:T(1,128)S(1)} %reshape.19.refs_1_, bf16[32,152,152]{2,1,0:T(8,128)(2,1)S(1)} %copy-done, s32[1,256]{1,0:T(1,128)S(1)} %bitcast.7, s32[1,256]{1,0:T(1,128)S(1)} %bitcast.5, bf16[8,152,152]{2,1,0:T(8,128)(2,1)S(1)} %copy-done.1), custom_call_target="tpu_custom_call" | custom-call | flops 1000000000 | bytes 8388608 | tf_op jit(solution)/shard_map/down/pallas_call | solution.py:412
  75.1 0.0 collective-permute-done.1.refs_3_
  75.1 0.0 collective-permute-done.2.refs_4_
  75.1 0.0 collective-permute-done.4.refs_6_
  75.1 5.1 %collective-permute-done.5.refs_7_ = bf16[152,256]{1,0:T(8,128)(2,1)} collective-permute-done((bf16[152,256]{1,0:T(8,128)(2,1)}, bf16[152,256]{1,0:T(8,128)(2,1)}, u32[]{:S(2)}, u32[]{:S(2)}) %collective-permute-start.5) | collective-permute-done | bytes 77856 | tf_op jit(solution)/shard_map/ppermute | solution.py:40
  80.3 51.8 %far.1 = bf16[152,2048]{1,0:T(8,128)(2,1)} custom-call(s32[32,2048]{1,0:T(8,128)S(1)} %copy-done.4, f32[4096,128]{1,0:T(8,128)S(1)} %copy-done.8, bf16[152,256]{1,0:T(8,128)(2,1)S(1)} %copy-done.6, bf16[152,256]{1,0:T(8,128)(2,1)} %collective-permute-done.1.refs_3_, bf16[152,256]{1,0:T(8,128)(2,1)} %collective-permute-done.2.refs_4_, ...), custom_call_target="tpu_custom_call" | custom-call | flops 40000000000 | bytes 16777216 | tf_op jit(solution)/shard_map/far/pallas_call | solution.py:424
  (19 shorter events, 0.0 us)
Async XLA Ops:
  0.0 68.9 %copy-start.9 = (s32[32,64]{1,0:T(8,128)S(1)}, s32[32,64]{1,0:T(8,128)}, u32[]{:S(2)}) copy-start(s32[32,64]{1,0:T(8,128)} %param.17) | copy-start | bytes 24580
  0.0 71.8 %copy-start = (bf16[32,152,152]{2,1,0:T(8,128)(2,1)S(1)}, bf16[32,152,152]{2,1,0:T(8,128)(2,1)}, u32[]{:S(2)}) copy-start(bf16[32,152,152]{2,1,0:T(8,128)(2,1)} %refs_8_.1) | copy-start | bytes 4435972
  0.0 71.8 %copy-start.1 = (bf16[8,152,152]{2,1,0:T(8,128)(2,1)S(1)}, bf16[8,152,152]{2,1,0:T(8,128)(2,1)}, u32[]{:S(2)}) copy-start(bf16[8,152,152]{2,1,0:T(8,128)(2,1)} %refs_5_.1) | copy-start | bytes 1108996
  0.0 71.8 %copy-start.2 = (s32[256]{0:T(256)S(1)}, s32[256]{0:T(256)}, u32[]{:S(2)}) copy-start(s32[256]{0:T(256)} %param.15) | copy-start | bytes 3076
  0.0 71.8 %copy-start.3 = (s32[256]{0:T(256)S(1)}, s32[256]{0:T(256)}, u32[]{:S(2)}) copy-start(s32[256]{0:T(256)} %param.16) | copy-start | bytes 3076
  21.4 30.9 %all-to-all-start.1 = ((f32[32,8,128]{2,1,0:T(8,128)}), f32[32,8,128]{2,1,0:T(8,128)S(1)}, u32[]{:S(2)}, u32[]{:S(2)}) async-start(f32[32,8,128]{2,1,0:T(8,128)} %sum_over_y.1), calls=%async_computation.1 | async-start | bytes 262144 | tf_op jit(solution)/shard_map/all_to_all | solution.py:405
  35.2 33.9 %collective-permute-start = (bf16[152,256]{1,0:T(8,128)(2,1)}, bf16[152,256]{1,0:T(8,128)(2,1)S(1)}, u32[]{:S(2)}, u32[]{:S(2)}) collective-permute-start(bf16[152,256]{1,0:T(8,128)(2,1)} %get-tuple-element.14), channel_id=1, source_target_pairs={{12,0},{16,4},{20,8},{24,12},{28,16},{32,20},{36,24},{40,28},{44,3... | collective-permute-start | bytes 233480 | tf_op jit(solution)/shard_map/ppermute | solution.py:40
  53.0 18.8 %all-to-all-start.2 = ((f32[16,8,128]{2,1,0:T(8,128)}), f32[16,8,128]{2,1,0:T(8,128)S(1)}, u32[]{:S(2)}, u32[]{:S(2)}) async-start(f32[16,8,128]{2,1,0:T(8,128)} %sum_over_z.1), calls=%async_computation.2 | async-start | bytes 131072 | tf_op jit(solution)/shard_map/all_to_all | solution.py:409
  58.7 16.4 %collective-permute-start.1 = (bf16[152,256]{1,0:T(8,128)(2,1)}, bf16[152,256]{1,0:T(8,128)(2,1)}, u32[]{:S(2)}, u32[]{:S(2)}) collective-permute-start(bf16[152,256]{1,0:T(8,128)(2,1)} %get-tuple-element.15), channel_id=1, source_target_pairs={{8,0},{12,4},{16,8},{20,12},{24,16},{28,20},{32,24},{36,28},{40,32... | collective-permute-start | bytes 233480 | tf_op jit(solution)/shard_map/ppermute | solution.py:40
  60.7 14.5 %collective-permute-start.2 = (bf16[152,256]{1,0:T(8,128)(2,1)}, bf16[152,256]{1,0:T(8,128)(2,1)}, u32[]{:S(2)}, u32[]{:S(2)}) collective-permute-start(bf16[152,256]{1,0:T(8,128)(2,1)} %get-tuple-element.16), channel_id=1, source_target_pairs={{4,0},{8,4},{12,8},{16,12},{20,16},{24,20},{28,24},{32,28},{36,32}... | collective-permute-start | bytes 233480 | tf_op jit(solution)/shard_map/ppermute | solution.py:40
  62.6 12.5 %collective-permute-start.3 = (bf16[152,256]{1,0:T(8,128)(2,1)}, bf16[152,256]{1,0:T(8,128)(2,1)}, u32[]{:S(2)}, u32[]{:S(2)}) collective-permute-start(bf16[152,256]{1,0:T(8,128)(2,1)} %get-tuple-element.17), channel_id=1, source_target_pairs={{0,4},{4,8},{8,12},{12,16},{16,20},{20,24},{24,28},{28,32},{32,36}... | collective-permute-start | bytes 233480 | tf_op jit(solution)/shard_map/ppermute | solution.py:40
  65.0 10.1 %collective-permute-start.4 = (bf16[152,256]{1,0:T(8,128)(2,1)}, bf16[152,256]{1,0:T(8,128)(2,1)}, u32[]{:S(2)}, u32[]{:S(2)}) collective-permute-start(bf16[152,256]{1,0:T(8,128)(2,1)} %get-tuple-element.18), channel_id=1, source_target_pairs={{0,8},{4,12},{8,16},{12,20},{16,24},{20,28},{24,32},{28,36},{32,40... | collective-permute-start | bytes 233480 | tf_op jit(solution)/shard_map/ppermute | solution.py:40
  69.0 0.6 copy-start.5
  69.7 10.6 %copy-start.4 = (s32[32,2048]{1,0:T(8,128)S(1)}, s32[32,2048]{1,0:T(8,128)}, u32[]{:S(2)}) copy-start(s32[32,2048]{1,0:T(8,128)} %refs_0_.1) | copy-start | bytes 786436
  69.7 10.6 %copy-start.7 = (s32[2048]{0:T(1024)S(1)}, s32[2048]{0:T(1024)}, u32[]{:S(2)}) copy-start(s32[2048]{0:T(1024)} %param.12) | copy-start | bytes 24580
  69.7 10.6 %collective-permute-start.5 = (bf16[152,256]{1,0:T(8,128)(2,1)}, bf16[152,256]{1,0:T(8,128)(2,1)}, u32[]{:S(2)}, u32[]{:S(2)}) collective-permute-start(bf16[152,256]{1,0:T(8,128)(2,1)} %get-tuple-element.19), channel_id=1, source_target_pairs={{0,12},{4,16},{8,20},{12,24},{16,28},{20,32},{24,36},{28,40},{32,4... | collective-permute-start | bytes 233480 | tf_op jit(solution)/shard_map/ppermute | solution.py:40
  71.9 8.4 %copy-start.6 = (bf16[152,256]{1,0:T(8,128)(2,1)S(1)}, bf16[152,256]{1,0:T(8,128)(2,1)}, u32[]{:S(2)}) copy-start(bf16[152,256]{1,0:T(8,128)(2,1)} %copy-done.5) | copy-start | bytes 233476
  71.9 8.4 %copy-start.8 = (f32[4096,128]{1,0:T(8,128)S(1)}, f32[4096,128]{1,0:T(8,128)}, u32[]{:S(2)}) copy-start(f32[4096,128]{1,0:T(8,128)} %get-tuple-element.13.refs_1_) | copy-start | bytes 6291460

commit v4 on v3

--- a/solution.py
+++ b/solution.py
@@ -401,11 +401,15 @@
         name="local",
     )(leaf_mult, occ, ghost_rows, code, group_of, m2m, coarse_up)
     slices = partial.reshape(near_devices, LANES // near_devices, 2 * COARSE)
-    for group, following in ((NEAR, OTHER), (OTHER, NEAR)):
-        slices = lax.all_to_all(slices, group, 0, 0, tiled=True)
-        slices = summed_parts(slices, lax.axis_size(following), "sum_over_" + group[0])
+    slices = lax.all_to_all(slices, NEAR, 0, 0, tiled=True)
+    slices = summed_parts(slices, lax.axis_size(OTHER), "sum_over_y")
+    packets, slices = lax.optimization_barrier((packets, slices))
+    slices = lax.all_to_all(slices, OTHER, 0, 0, tiled=True)
     stride_list = [stride for stride in range(-REACH, REACH + 1) if stride != 0]
     ghosts = [passed_along(packets[n], CURVE, stride) for n, stride in enumerate(stride_list)]
+    first_ghosts, slices = lax.optimization_barrier((ghosts[:-1], slices))
+    ghosts = [*first_ghosts, ghosts[-1]]
+    slices = summed_parts(slices, near_devices, "sum_over_z")
     everywhere = lax.all_to_all(slices, NEAR, 0, 0, tiled=True)
     wanted = coarse_list.reshape(1, -1)
     sources = (everywhere, wanted, m2l, group_of, code, l2l)

time: 132 us -> 132 us (level)
  the two profiles are of different devices: /device:TPU:10 before, /device:TPU:1 now
where the time goes in v4:
time: 132 us
  Pallas kernels  62.9 us (48%)
  starting transfers between devices  42.4 us (32%)
  blocking collectives  14.1 us (11%)
  local copies, waits for them, and re-layouts  7.66 us (6%)
  waiting for transfers between devices  4.37 us (3%)
    pallas_call x1, Pallas kernels, shards(): pl.pallas_call(far_kernel, out_shape=shape((points, slots), BF16), in_spe...  52.2 us
    all_to_all x1, starting transfers between devices, shards(): slices = lax.all_to_all(slices, OTHER, 0, 0, tiled=True)  17.4 us
    ppermute x6, starting transfers between devices, passed_along(): return lax.ppermute(block, axis, route)  14.9 us
    all_to_all x1, blocking collectives, shards(): slices = lax.all_to_all(slices, NEAR, 0, 0, tiled=True)  14.1 us
    all_to_all x1, starting transfers between devices, shards(): everywhere = lax.all_to_all(slices, NEAR, 0, 0, tiled=True)  10.1 us
    unnamed x36, local copies, waits for them, and re-layouts  7.58 us
    pallas_call x1, Pallas kernels, shards(): pl.pallas_call(local_kernel, out_shape=[shape((2 * slots, LANES), F32), s...  6.21 us
    all_to_all x1, waiting for transfers between devices, shards(): everywhere = lax.all_to_all(slices, NEAR, 0, 0, tiled=True)  4.36 us
  transfers between devices with their start and end apart: 8, of which 1 were waited for; matrix products, arithmetic and copies ran while one was open for 0% of the time, Pallas kernels for 2%

profile of v4, /device:TPU:1, one launch (start us, length us, event | category | flops | bytes accessed | tf_op | source)
XLA Modules:
  0.0 131.6 jit_solution(1564390848630602598)
XLA Ops:
  0.0 6.2 %local.1 = (f32[4096,128]{1,0:T(8,128)}, f32[128,128]{1,0:T(8,128)}, bf16[152,256]{1,0:T(8,128)(2,1)}, bf16[152,256]{1,0:T(8,128)(2,1)}, bf16[152,256]{1,0:T(8,1...) custom-call(bf16[152,2048]{1,0:T(8,128)(2,1)} %leaf_hbm.1, ...), custom_call_target="tpu_custom_call" | custom-call | flops 1000000000 | bytes 4194304 | tf_op jit(solution)/shard_map/local/pallas_call | solution.py:379
  6.3 14.1 %all_to_all.15.parts_ref = f32[16,8,128]{2,1,0:T(8,128)S(1)} all-to-all(f32[16,8,128]{2,1,0:T(8,128)} %bitcast.10), channel_id=1, replica_groups=mesh['y'=4,'z'=16,'core'=2,'oct'=4] {'y','oct'}, dimensions={0} | all-to-all | bytes 131072 | tf_op jit(solution)/shard_map/all_to_all | solution.py:404
  20.4 0.7 sum_over_y.1
  21.0 17.4 %all-to-all-start.1 = ((f32[32,8,128]{2,1,0:T(8,128)}), f32[32,8,128]{2,1,0:T(8,128)S(1)}, u32[]{:S(2)}, u32[]{:S(2)}) async-start(f32[32,8,128]{2,1,0:T(8,128)} %sum_over_y.1), calls=%async_computation.1 | async-start | bytes 262144 | tf_op jit(solution)/shard_map/all_to_all | solution.py:407
  38.4 1.3 collective-permute-start
  39.7 1.3 collective-permute-start.1
  41.0 2.1 %collective-permute-start.2 = (bf16[152,256]{1,0:T(8,128)(2,1)}, bf16[152,256]{1,0:T(8,128)(2,1)S(1)}, u32[]{:S(2)}, u32[]{:S(2)}) collective-permute-start(bf16[152,256]{1,0:T(8,128)(2,1)} %get-tuple-element.36), channel_id=1, source_target_pairs={{4,0},{8,4},{12,8},{16,12},{20,16},{24,20},{28,24},{32,28},{36,32}... | collective-permute-start | bytes 233480 | tf_op jit(solution)/shard_map/ppermute | solution.py:40
  43.2 4.2 %collective-permute-start.3 = (bf16[152,256]{1,0:T(8,128)(2,1)}, bf16[152,256]{1,0:T(8,128)(2,1)S(1)}, u32[]{:S(2)}, u32[]{:S(2)}) collective-permute-start(bf16[152,256]{1,0:T(8,128)(2,1)} %get-tuple-element.37), channel_id=1, source_target_pairs={{0,4},{4,8},{8,12},{12,16},{16,20},{20,24},{24,28},{28,32},{32,36}... | collective-permute-start | bytes 233480 | tf_op jit(solution)/shard_map/ppermute | solution.py:40
  47.3 4.0 %collective-permute-start.4 = (bf16[152,256]{1,0:T(8,128)(2,1)}, bf16[152,256]{1,0:T(8,128)(2,1)S(1)}, u32[]{:S(2)}, u32[]{:S(2)}) collective-permute-start(bf16[152,256]{1,0:T(8,128)(2,1)} %get-tuple-element.38), channel_id=1, source_target_pairs={{0,8},{4,12},{8,16},{12,20},{16,24},{20,28},{24,32},{28,36},{32,40... | collective-permute-start | bytes 233480 | tf_op jit(solution)/shard_map/ppermute | solution.py:40
  51.3 0.6 copy-done.5
  52.0 0.6 copy-done.7
  52.6 0.6 copy-done.9
  53.9 0.6 copy-done.13
  54.5 0.7 sum_over_z.1
  55.2 10.1 %all-to-all-start.2 = ((f32[16,8,128]{2,1,0:T(8,128)}), f32[16,8,128]{2,1,0:T(8,128)S(1)}, u32[]{:S(2)}, u32[]{:S(2)}) async-start(f32[16,8,128]{2,1,0:T(8,128)} %sum_over_z.1), calls=%async_computation.2 | async-start | bytes 131072 | tf_op jit(solution)/shard_map/all_to_all | solution.py:413
  65.4 2.1 %collective-permute-start.5 = (bf16[152,256]{1,0:T(8,128)(2,1)}, bf16[152,256]{1,0:T(8,128)(2,1)}, u32[]{:S(2)}, u32[]{:S(2)}) collective-permute-start(bf16[152,256]{1,0:T(8,128)(2,1)} %get-tuple-element.45), channel_id=1, source_target_pairs={{0,12},{4,16},{8,20},{12,24},{16,28},{20,32},{24,36},{28,40},{32,4... | collective-permute-start | bytes 233480 | tf_op jit(solution)/shard_map/ppermute | solution.py:40
  67.4 4.4 %all-to-all-done.2.refs_0_ = f32[16,8,128]{2,1,0:T(8,128)S(1)} async-done(((f32[16,8,128]{2,1,0:T(8,128)}), f32[16,8,128]{2,1,0:T(8,128)S(1)}, u32[]{:S(2)}, u32[]{:S(2)}) %all-to-all-start.2) | async-done | bytes 65568 | tf_op jit(solution)/shard_map/all_to_all | solution.py:413
  71.8 3.2 %down.1.refs_10_ = f32[4096,128]{1,0:T(8,128)S(1)} custom-call(f32[16,8,128]{2,1,0:T(8,128)S(1)} %all-to-all-done.2.refs_0_, s32[1,2048]{1,0:T(1,128)S(1)} %reshape.19.refs_1_, bf16[32,152,152]{2,1,0:T(8,128)(2,1)S(1)} %copy-done, s32[1,256]{1,0:T(1,128)S(1)} %bitcast.7, s32[1,256]{1,0:T(1,128)S(1)} %bitcast.5, bf16[8,152,152]{2,1,0:T(8,128)(2,1)S(1)} %copy-done.1), custom_call_target="tpu_custom_call" | custom-call | flops 1000000000 | bytes 8388608 | tf_op jit(solution)/shard_map/down/pallas_call | solution.py:416
  75.1 0.9 copy-done.6
  76.0 0.9 copy-done.8
  76.8 0.9 copy-done.10
  77.7 0.9 copy-done.12
  78.6 0.9 copy-done.14
  79.5 52.2 %far.1 = bf16[152,2048]{1,0:T(8,128)(2,1)} custom-call(s32[32,2048]{1,0:T(8,128)S(1)} %copy-done.4, f32[4096,128]{1,0:T(8,128)S(1)} %copy-done.16, bf16[152,256]{1,0:T(8,128)(2,1)S(1)} %copy-done.6, bf16[152,256]{1,0:T(8,128)(2,1)S(1)} %copy-done.8, bf16[152,256]{1,0:T(8,128)(2,1)S(1)} %copy-done.10, bf16[152,256]{1,0:T(8,128)(2,1)S(1)} %copy-done.12, ...), custom_call_target="tpu_custom_call" | custom-call | flops 40000000000 | bytes 16777216 | tf_op jit(solution)/shard_map/far/pallas_call | solution.py:428
  (35 shorter events, 0.8 us)
Async XLA Ops:
  0.0 65.3 %copy-start.17 = (s32[32,64]{1,0:T(8,128)S(1)}, s32[32,64]{1,0:T(8,128)}, u32[]{:S(2)}) copy-start(s32[32,64]{1,0:T(8,128)} %param.17) | copy-start | bytes 24580
  0.0 71.8 %copy-start = (bf16[32,152,152]{2,1,0:T(8,128)(2,1)S(1)}, bf16[32,152,152]{2,1,0:T(8,128)(2,1)}, u32[]{:S(2)}) copy-start(bf16[32,152,152]{2,1,0:T(8,128)(2,1)} %refs_8_.1) | copy-start | bytes 4435972
  0.0 71.8 %copy-start.1 = (bf16[8,152,152]{2,1,0:T(8,128)(2,1)S(1)}, bf16[8,152,152]{2,1,0:T(8,128)(2,1)}, u32[]{:S(2)}) copy-start(bf16[8,152,152]{2,1,0:T(8,128)(2,1)} %refs_5_.1) | copy-start | bytes 1108996
  0.0 71.8 %copy-start.2 = (s32[256]{0:T(256)S(1)}, s32[256]{0:T(256)}, u32[]{:S(2)}) copy-start(s32[256]{0:T(256)} %param.15) | copy-start | bytes 3076
  0.0 71.8 %copy-start.3 = (s32[256]{0:T(256)S(1)}, s32[256]{0:T(256)}, u32[]{:S(2)}) copy-start(s32[256]{0:T(256)} %param.16) | copy-start | bytes 3076
  21.0 33.4 %all-to-all-start.1 = ((f32[32,8,128]{2,1,0:T(8,128)}), f32[32,8,128]{2,1,0:T(8,128)S(1)}, u32[]{:S(2)}, u32[]{:S(2)}) async-start(f32[32,8,128]{2,1,0:T(8,128)} %sum_over_y.1), calls=%async_computation.1 | async-start | bytes 262144 | tf_op jit(solution)/shard_map/all_to_all | solution.py:407
  38.4 12.9 %collective-permute-start = (bf16[152,256]{1,0:T(8,128)(2,1)}, bf16[152,256]{1,0:T(8,128)(2,1)S(1)}, u32[]{:S(2)}, u32[]{:S(2)}) collective-permute-start(bf16[152,256]{1,0:T(8,128)(2,1)} %get-tuple-element.34), channel_id=1, source_target_pairs={{12,0},{16,4},{20,8},{24,12},{28,16},{32,20},{36,24},{40,28},{44,3... | collective-permute-start | bytes 233480 | tf_op jit(solution)/shard_map/ppermute | solution.py:40
  39.7 12.3 %collective-permute-start.1 = (bf16[152,256]{1,0:T(8,128)(2,1)}, bf16[152,256]{1,0:T(8,128)(2,1)S(1)}, u32[]{:S(2)}, u32[]{:S(2)}) collective-permute-start(bf16[152,256]{1,0:T(8,128)(2,1)} %get-tuple-element.35), channel_id=1, source_target_pairs={{8,0},{12,4},{16,8},{20,12},{24,16},{28,20},{32,24},{36,28},{40,32... | collective-permute-start | bytes 233480 | tf_op jit(solution)/shard_map/ppermute | solution.py:40
  41.0 11.6 %collective-permute-start.2 = (bf16[152,256]{1,0:T(8,128)(2,1)}, bf16[152,256]{1,0:T(8,128)(2,1)S(1)}, u32[]{:S(2)}, u32[]{:S(2)}) collective-permute-start(bf16[152,256]{1,0:T(8,128)(2,1)} %get-tuple-element.36), channel_id=1, source_target_pairs={{4,0},{8,4},{12,8},{16,12},{20,16},{24,20},{28,24},{32,28},{36,32}... | collective-permute-start | bytes 233480 | tf_op jit(solution)/shard_map/ppermute | solution.py:40
  43.2 10.1 %collective-permute-start.3 = (bf16[152,256]{1,0:T(8,128)(2,1)}, bf16[152,256]{1,0:T(8,128)(2,1)S(1)}, u32[]{:S(2)}, u32[]{:S(2)}) collective-permute-start(bf16[152,256]{1,0:T(8,128)(2,1)} %get-tuple-element.37), channel_id=1, source_target_pairs={{0,4},{4,8},{8,12},{12,16},{16,20},{20,24},{24,28},{28,32},{32,36}... | collective-permute-start | bytes 233480 | tf_op jit(solution)/shard_map/ppermute | solution.py:40
  47.3 6.5 %collective-permute-start.4 = (bf16[152,256]{1,0:T(8,128)(2,1)}, bf16[152,256]{1,0:T(8,128)(2,1)S(1)}, u32[]{:S(2)}, u32[]{:S(2)}) collective-permute-start(bf16[152,256]{1,0:T(8,128)(2,1)} %get-tuple-element.38), channel_id=1, source_target_pairs={{0,8},{4,12},{8,16},{12,20},{16,24},{20,28},{24,32},{28,36},{32,40... | collective-permute-start | bytes 233480 | tf_op jit(solution)/shard_map/ppermute | solution.py:40
  51.3 0.6 copy-start.5
  52.0 0.6 copy-start.7
  53.9 0.6 copy-start.13
  55.2 16.6 %all-to-all-start.2 = ((f32[16,8,128]{2,1,0:T(8,128)}), f32[16,8,128]{2,1,0:T(8,128)S(1)}, u32[]{:S(2)}, u32[]{:S(2)}) async-start(f32[16,8,128]{2,1,0:T(8,128)} %sum_over_z.1), calls=%async_computation.2 | async-start | bytes 131072 | tf_op jit(solution)/shard_map/all_to_all | solution.py:413
  65.4 9.7 %copy-start.4 = (s32[32,2048]{1,0:T(8,128)S(1)}, s32[32,2048]{1,0:T(8,128)}, u32[]{:S(2)}) copy-start(s32[32,2048]{1,0:T(8,128)} %refs_0_.1) | copy-start | bytes 786436
  65.4 9.7 %copy-start.15 = (s32[2048]{0:T(1024)S(1)}, s32[2048]{0:T(1024)}, u32[]{:S(2)}) copy-start(s32[2048]{0:T(1024)} %param.12) | copy-start | bytes 24580
  65.4 9.6 %collective-permute-start.5 = (bf16[152,256]{1,0:T(8,128)(2,1)}, bf16[152,256]{1,0:T(8,128)(2,1)}, u32[]{:S(2)}, u32[]{:S(2)}) collective-permute-start(bf16[152,256]{1,0:T(8,128)(2,1)} %get-tuple-element.45), channel_id=1, source_target_pairs={{0,12},{4,16},{8,20},{12,24},{16,28},{20,32},{24,36},{28,40},{32,4... | collective-permute-start | bytes 233480 | tf_op jit(solution)/shard_map/ppermute | solution.py:40
  71.8 3.2 %copy-start.16 = (f32[4096,128]{1,0:T(8,128)S(1)}, f32[4096,128]{1,0:T(8,128)}, u32[]{:S(2)}) copy-start(f32[4096,128]{1,0:T(8,128)} %get-tuple-element.26.refs_1_) | copy-start | bytes 6291460
  75.1 0.9 copy-start.6
  75.9 0.9 copy-start.8
  76.8 0.9 copy-start.10
  77.7 0.9 copy-start.12
  78.6 0.9 copy-start.14
  (2 other events, 1.2 us)

commit v5 on v4

--- a/solution.py
+++ b/solution.py
@@ -13,7 +13,7 @@
 TILE = 256
 DEPTH = 2
 PART = 80
-FAR_MIB = 40
+FAR_MIB = 60
 NEAR = ("y", "oct")
 OTHER = ("z", "core")
 CURVE = ("y", "z", "core")

time: 132 us -> 129 us (0.977)
  local copies, waits for them, and re-layouts: 7.66 us -> 2.72 us
  waiting for transfers between devices: 4.37 us -> 6.72 us
    unnamed x36 -> x22, local copies, waits for them, and re-layouts: 7.58 us -> 2.64 us
  transfers between devices with their start and end apart: 8 -> 8, of which waited for: 1 -> 3; matrix products, arithmetic and copies ran while one was open for 0% -> 0% of each run, Pallas kernels for 2% -> 2%
where the time goes in v5:
time: 129 us
  Pallas kernels  62.9 us (49%)
  starting transfers between devices  42 us (33%)
  blocking collectives  14.1 us (11%)
  waiting for transfers between devices  6.72 us (5%)
  local copies, waits for them, and re-layouts  2.72 us (2%)
    pallas_call x1, Pallas kernels, shards(): pl.pallas_call(far_kernel, out_shape=shape((points, slots), BF16), in_spe...  52.1 us
    all_to_all x1, starting transfers between devices, shards(): slices = lax.all_to_all(slices, OTHER, 0, 0, tiled=True)  17.4 us
    ppermute x6, starting transfers between devices, passed_along(): return lax.ppermute(block, axis, route)  14.8 us
    all_to_all x1, blocking collectives, shards(): slices = lax.all_to_all(slices, NEAR, 0, 0, tiled=True)  14.1 us
    all_to_all x1, starting transfers between devices, shards(): everywhere = lax.all_to_all(slices, NEAR, 0, 0, tiled=True)  9.82 us
    pallas_call x1, Pallas kernels, shards(): pl.pallas_call(local_kernel, out_shape=[shape((2 * slots, LANES), F32), s...  6.22 us
    all_to_all x1, waiting for transfers between devices, shards(): everywhere = lax.all_to_all(slices, NEAR, 0, 0, tiled=True)  5.14 us
    pallas_call x1, Pallas kernels, shards(): pl.pallas_call(down_kernel, out_shape=shape((2 * slots, LANES), F32), in_...  3.19 us
  transfers between devices with their start and end apart: 8, of which 3 were waited for; matrix products, arithmetic and copies ran while one was open for 0% of the time, Pallas kernels for 2%

profile of v5, /device:TPU:1, one launch (start us, length us, event | category | flops | bytes accessed | tf_op | source)
XLA Modules:
  0.0 128.6 jit_solution(18065609591546308247)
XLA Ops:
  0.0 6.2 %local.1 = (f32[4096,128]{1,0:T(8,128)}, f32[128,128]{1,0:T(8,128)}, bf16[152,256]{1,0:T(8,128)(2,1)}, bf16[152,256]{1,0:T(8,128)(2,1)}, bf16[152,256]{1,0:T(8,1...) custom-call(bf16[152,2048]{1,0:T(8,128)(2,1)} %leaf_hbm.1, ...), custom_call_target="tpu_custom_call" | custom-call | flops 1000000000 | bytes 4194304 | tf_op jit(solution)/shard_map/local/pallas_call | solution.py:379
  6.3 14.1 %all_to_all.15.parts_ref = f32[16,8,128]{2,1,0:T(8,128)S(1)} all-to-all(f32[16,8,128]{2,1,0:T(8,128)} %bitcast.8), channel_id=1, replica_groups=mesh['y'=4,'z'=16,'core'=2,'oct'=4] {'y','oct'}, dimensions={0} | all-to-all | bytes 131072 | tf_op jit(solution)/shard_map/all_to_all | solution.py:404
  20.4 0.7 sum_over_y.1
  21.1 17.4 %all-to-all-start.1 = ((f32[32,8,128]{2,1,0:T(8,128)}), f32[32,8,128]{2,1,0:T(8,128)S(1)}, u32[]{:S(2)}, u32[]{:S(2)}) async-start(f32[32,8,128]{2,1,0:T(8,128)} %sum_over_y.1), calls=%async_computation.1 | async-start | bytes 262144 | tf_op jit(solution)/shard_map/all_to_all | solution.py:407
  38.4 1.3 %collective-permute-start = (bf16[152,256]{1,0:T(8,128)(2,1)}, bf16[152,256]{1,0:T(8,128)(2,1)S(1)}, u32[]{:S(2)}, u32[]{:S(2)}) collective-permute-start(bf16[152,256]{1,0:T(8,128)(2,1)} %get-tuple-element.34), channel_id=1, source_target_pairs={{12,0},{16,4},{20,8},{24,12},{28,16},{32,20},{36,24},{40,28},{44,3... | collective-permute-start | bytes 233480 | tf_op jit(solution)/shard_map/ppermute | solution.py:40
  39.7 1.3 %collective-permute-start.1 = (bf16[152,256]{1,0:T(8,128)(2,1)}, bf16[152,256]{1,0:T(8,128)(2,1)S(1)}, u32[]{:S(2)}, u32[]{:S(2)}) collective-permute-start(bf16[152,256]{1,0:T(8,128)(2,1)} %get-tuple-element.35), channel_id=1, source_target_pairs={{8,0},{12,4},{16,8},{20,12},{24,16},{28,20},{32,24},{36,28},{40,32... | collective-permute-start | bytes 233480 | tf_op jit(solution)/shard_map/ppermute | solution.py:40
  41.0 2.1 %collective-permute-start.2 = (bf16[152,256]{1,0:T(8,128)(2,1)}, bf16[152,256]{1,0:T(8,128)(2,1)S(1)}, u32[]{:S(2)}, u32[]{:S(2)}) collective-permute-start(bf16[152,256]{1,0:T(8,128)(2,1)} %get-tuple-element.36), channel_id=1, source_target_pairs={{4,0},{8,4},{12,8},{16,12},{20,16},{24,20},{28,24},{32,28},{36,32}... | collective-permute-start | bytes 233480 | tf_op jit(solution)/shard_map/ppermute | solution.py:40
  43.2 4.2 %collective-permute-start.3 = (bf16[152,256]{1,0:T(8,128)(2,1)}, bf16[152,256]{1,0:T(8,128)(2,1)S(1)}, u32[]{:S(2)}, u32[]{:S(2)}) collective-permute-start(bf16[152,256]{1,0:T(8,128)(2,1)} %get-tuple-element.37), channel_id=1, source_target_pairs={{0,4},{4,8},{8,12},{12,16},{16,20},{20,24},{24,28},{28,32},{32,36}... | collective-permute-start | bytes 233480 | tf_op jit(solution)/shard_map/ppermute | solution.py:40
  47.3 4.6 %collective-permute-start.4 = (bf16[152,256]{1,0:T(8,128)(2,1)}, bf16[152,256]{1,0:T(8,128)(2,1)}, u32[]{:S(2)}, u32[]{:S(2)}) collective-permute-start(bf16[152,256]{1,0:T(8,128)(2,1)} %get-tuple-element.38), channel_id=1, source_target_pairs={{0,8},{4,12},{8,16},{12,20},{16,24},{20,28},{24,32},{28,36},{32,40... | collective-permute-start | bytes 233480 | tf_op jit(solution)/shard_map/ppermute | solution.py:40
  52.0 0.0 collective-permute-done.1.refs_3_
  52.0 0.0 collective-permute-done.2.refs_4_
  52.0 0.7 copy-done.9
  52.7 0.4 collective-permute-done.4.refs_6_
  53.1 1.2 all-to-all-done.1.parts_ref
  54.3 0.7 sum_over_z.1
  54.9 9.8 %all-to-all-start.2 = ((f32[16,8,128]{2,1,0:T(8,128)}), f32[16,8,128]{2,1,0:T(8,128)S(1)}, u32[]{:S(2)}, u32[]{:S(2)}) async-start(f32[16,8,128]{2,1,0:T(8,128)} %sum_over_z.1), calls=%async_computation.2 | async-start | bytes 131072 | tf_op jit(solution)/shard_map/all_to_all | solution.py:413
  64.8 0.1 reshape.19.refs_1_
  64.8 1.3 collective-permute-start.5
  66.1 5.1 %all-to-all-done.2.refs_0_ = f32[16,8,128]{2,1,0:T(8,128)S(1)} async-done(((f32[16,8,128]{2,1,0:T(8,128)}), f32[16,8,128]{2,1,0:T(8,128)S(1)}, u32[]{:S(2)}, u32[]{:S(2)}) %all-to-all-start.2) | async-done | bytes 65568 | tf_op jit(solution)/shard_map/all_to_all | solution.py:413
  71.3 3.2 %down.1.refs_10_ = f32[4096,128]{1,0:T(8,128)S(1)} custom-call(f32[16,8,128]{2,1,0:T(8,128)S(1)} %all-to-all-done.2.refs_0_, s32[1,2048]{1,0:T(1,128)S(1)} %reshape.19.refs_1_, bf16[32,152,152]{2,1,0:T(8,128)(2,1)S(1)} %copy-done, s32[1,256]{1,0:T(1,128)S(1)} %bitcast.7, s32[1,256]{1,0:T(1,128)S(1)} %bitcast.5, bf16[8,152,152]{2,1,0:T(8,128)(2,1)S(1)} %copy-done.2), custom_call_target="tpu_custom_call" | custom-call | flops 1000000000 | bytes 8388608 | tf_op jit(solution)/shard_map/down/pallas_call | solution.py:416
  74.5 1.3 %copy-done.1 = f32[4096,128]{1,0:T(8,128)} copy-done((f32[4096,128]{1,0:T(8,128)}, f32[4096,128]{1,0:T(8,128)S(1)}, u32[]{:S(2)}) %copy-start.1) | copy-done | bytes 2097176
  75.8 0.0 collective-permute-done.5.refs_7_
  75.8 0.6 copy-done.10
  76.5 52.1 %far.1 = bf16[152,2048]{1,0:T(8,128)(2,1)} custom-call(s32[32,2048]{1,0:T(8,128)} %refs_0_.1, f32[4096,128]{1,0:T(8,128)} %get-tuple-element.26.refs_1_, bf16[152,256]{1,0:T(8,128)(2,1)} %copy-done.6, bf16[152,256]{1,0:T(8,128)(2,1)} %copy-done.7, bf16[152,256]{1,0:T(8,128)(2,1)} %copy-done.8, bf16[152,256]{1,0:T(8,128)(2,1)} %copy-done.9, ...), custom_call_target="tpu_custom_call" | custom-call | flops 40000000000 | bytes 16777216 | tf_op jit(solution)/shard_map/far/pallas_call | solution.py:428
  (21 shorter events, 0.0 us)
Async XLA Ops:
  0.0 64.8 %copy-start.5 = (s32[32,64]{1,0:T(8,128)S(1)}, s32[32,64]{1,0:T(8,128)}, u32[]{:S(2)}) copy-start(s32[32,64]{1,0:T(8,128)} %param.17) | copy-start | bytes 24580
  0.0 71.3 %copy-start = (bf16[32,152,152]{2,1,0:T(8,128)(2,1)S(1)}, bf16[32,152,152]{2,1,0:T(8,128)(2,1)}, u32[]{:S(2)}) copy-start(bf16[32,152,152]{2,1,0:T(8,128)(2,1)} %refs_8_.1) | copy-start | bytes 4435972
  0.0 71.3 %copy-start.2 = (bf16[8,152,152]{2,1,0:T(8,128)(2,1)S(1)}, bf16[8,152,152]{2,1,0:T(8,128)(2,1)}, u32[]{:S(2)}) copy-start(bf16[8,152,152]{2,1,0:T(8,128)(2,1)} %refs_5_.1) | copy-start | bytes 1108996
  0.0 71.3 %copy-start.3 = (s32[256]{0:T(256)S(1)}, s32[256]{0:T(256)}, u32[]{:S(2)}) copy-start(s32[256]{0:T(256)} %param.15) | copy-start | bytes 3076
  0.0 71.3 %copy-start.4 = (s32[256]{0:T(256)S(1)}, s32[256]{0:T(256)}, u32[]{:S(2)}) copy-start(s32[256]{0:T(256)} %param.16) | copy-start | bytes 3076
  21.1 33.2 %all-to-all-start.1 = ((f32[32,8,128]{2,1,0:T(8,128)}), f32[32,8,128]{2,1,0:T(8,128)S(1)}, u32[]{:S(2)}, u32[]{:S(2)}) async-start(f32[32,8,128]{2,1,0:T(8,128)} %sum_over_y.1), calls=%async_computation.1 | async-start | bytes 262144 | tf_op jit(solution)/shard_map/all_to_all | solution.py:407
  38.4 13.6 %collective-permute-start = (bf16[152,256]{1,0:T(8,128)(2,1)}, bf16[152,256]{1,0:T(8,128)(2,1)S(1)}, u32[]{:S(2)}, u32[]{:S(2)}) collective-permute-start(bf16[152,256]{1,0:T(8,128)(2,1)} %get-tuple-element.34), channel_id=1, source_target_pairs={{12,0},{16,4},{20,8},{24,12},{28,16},{32,20},{36,24},{40,28},{44,3... | collective-permute-start | bytes 233480 | tf_op jit(solution)/shard_map/ppermute | solution.py:40
  39.7 12.3 %collective-permute-start.1 = (bf16[152,256]{1,0:T(8,128)(2,1)}, bf16[152,256]{1,0:T(8,128)(2,1)S(1)}, u32[]{:S(2)}, u32[]{:S(2)}) collective-permute-start(bf16[152,256]{1,0:T(8,128)(2,1)} %get-tuple-element.35), channel_id=1, source_target_pairs={{8,0},{12,4},{16,8},{20,12},{24,16},{28,20},{32,24},{36,28},{40,32... | collective-permute-start | bytes 233480 | tf_op jit(solution)/shard_map/ppermute | solution.py:40
  41.0 11.0 %collective-permute-start.2 = (bf16[152,256]{1,0:T(8,128)(2,1)}, bf16[152,256]{1,0:T(8,128)(2,1)S(1)}, u32[]{:S(2)}, u32[]{:S(2)}) collective-permute-start(bf16[152,256]{1,0:T(8,128)(2,1)} %get-tuple-element.36), channel_id=1, source_target_pairs={{4,0},{8,4},{12,8},{16,12},{20,16},{24,20},{28,24},{32,28},{36,32}... | collective-permute-start | bytes 233480 | tf_op jit(solution)/shard_map/ppermute | solution.py:40
  43.2 8.8 %collective-permute-start.3 = (bf16[152,256]{1,0:T(8,128)(2,1)}, bf16[152,256]{1,0:T(8,128)(2,1)S(1)}, u32[]{:S(2)}, u32[]{:S(2)}) collective-permute-start(bf16[152,256]{1,0:T(8,128)(2,1)} %get-tuple-element.37), channel_id=1, source_target_pairs={{0,4},{4,8},{8,12},{12,16},{16,20},{20,24},{24,28},{28,32},{32,36}... | collective-permute-start | bytes 233480 | tf_op jit(solution)/shard_map/ppermute | solution.py:40
  47.3 5.7 %collective-permute-start.4 = (bf16[152,256]{1,0:T(8,128)(2,1)}, bf16[152,256]{1,0:T(8,128)(2,1)}, u32[]{:S(2)}, u32[]{:S(2)}) collective-permute-start(bf16[152,256]{1,0:T(8,128)(2,1)} %get-tuple-element.38), channel_id=1, source_target_pairs={{0,8},{4,12},{8,16},{12,20},{16,24},{20,28},{24,32},{28,36},{32,40... | collective-permute-start | bytes 233480 | tf_op jit(solution)/shard_map/ppermute | solution.py:40
  52.0 22.5 %copy-start.6 = (bf16[152,256]{1,0:T(8,128)(2,1)}, bf16[152,256]{1,0:T(8,128)(2,1)S(1)}, u32[]{:S(2)}) copy-start(bf16[152,256]{1,0:T(8,128)(2,1)S(1)} %collective-permute-done.refs_2_) | copy-start | bytes 233476
  52.0 22.5 %copy-start.7 = (bf16[152,256]{1,0:T(8,128)(2,1)}, bf16[152,256]{1,0:T(8,128)(2,1)S(1)}, u32[]{:S(2)}) copy-start(bf16[152,256]{1,0:T(8,128)(2,1)S(1)} %collective-permute-done.1.refs_3_) | copy-start | bytes 233476
  52.0 22.5 %copy-start.8 = (bf16[152,256]{1,0:T(8,128)(2,1)}, bf16[152,256]{1,0:T(8,128)(2,1)S(1)}, u32[]{:S(2)}) copy-start(bf16[152,256]{1,0:T(8,128)(2,1)S(1)} %collective-permute-done.2.refs_4_) | copy-start | bytes 233476
  52.0 0.7 copy-start.9
  54.9 16.3 %all-to-all-start.2 = ((f32[16,8,128]{2,1,0:T(8,128)}), f32[16,8,128]{2,1,0:T(8,128)S(1)}, u32[]{:S(2)}, u32[]{:S(2)}) async-start(f32[16,8,128]{2,1,0:T(8,128)} %sum_over_z.1), calls=%async_computation.2 | async-start | bytes 131072 | tf_op jit(solution)/shard_map/all_to_all | solution.py:413
  64.8 11.0 %collective-permute-start.5 = (bf16[152,256]{1,0:T(8,128)(2,1)}, bf16[152,256]{1,0:T(8,128)(2,1)S(1)}, u32[]{:S(2)}, u32[]{:S(2)}) collective-permute-start(bf16[152,256]{1,0:T(8,128)(2,1)} %get-tuple-element.45), channel_id=1, source_target_pairs={{0,12},{4,16},{8,20},{12,24},{16,28},{20,32},{24,36},{28,40},{32,4... | collective-permute-start | bytes 233480 | tf_op jit(solution)/shard_map/ppermute | solution.py:40
  74.5 1.3 %copy-start.1 = (f32[4096,128]{1,0:T(8,128)}, f32[4096,128]{1,0:T(8,128)S(1)}, u32[]{:S(2)}) copy-start(f32[4096,128]{1,0:T(8,128)S(1)} %down.1.refs_10_) | copy-start | bytes 6291460
  75.8 0.6 copy-start.10
